TPU v7x, 256 devices: a whole 4x4x8 slice. The times are simulated.
256 devices in a mesh: row: 64 (over z, y, x_hi), col: 2 (over core), layer: 2 (over x_lo).
Axes of the slice: x: 4 (x_hi: 2, x_lo: 2; x = x_hi * 2 + x_lo), y: 4, z: 8, core: 2. Of those that a mesh axis runs over, the one named last changes fastest.
Arguments:
- a_blocks: bfloat16 [64, 128, 64, 64], P('row', ('col', 'layer')), may hold values from -6 to 6
- a_index: int32 [64, 128, 2], P('row', ('col', 'layer')), may hold values from 0 to 511, as said below
- a_count: int32 [64, 4], P('row', ('col', 'layer')), may hold values from 1 to 32, as said below
- b_blocks: bfloat16 [512, 2, 64, 64], P(('row', 'layer'), 'col'), may hold values from -0.75 to 0.75
- b_index: int32 [512, 2, 2], P(('row', 'layer'), 'col'), may hold values from 0 to 15, as said below
- b_count: int32 [128, 2], P(('row', 'layer'), 'col'), may hold values from 1 to 4, as said below
Outputs:
- product: bfloat16 [32768, 1024], P(('row', 'layer'), 'col')
Inputs may be any that keep to these rules, and one draw needn't show every extreme that they name: `a_index`: within one piece the live slots name distinct (block row, inner block) positions; entry 0 is below 8, entry 1 below 512. `b_index`: within one piece the live slots name distinct (inner block, block column) positions; entry 0 is below 16, entry 1 below 8. `a_count`: some piece is full. `b_count`: some piece is full.
All inputs are finite; a program needn't handle non-finite values.
Results may differ from a plain program's by a relative error of at most 0.001.
Values may be sent and summed in bfloat16 or wider, within the bound.
No kernel may reach another device: no remote copies, remote signals or barrier semaphores. Data moves between devices by JAX's collectives and lax.ppermute only.
A program may use at most 128 MiB of HBM per device.

v0:
```python
import functools

import jax
import jax.numpy as jnp
from jax import lax
from jax.experimental import pallas as pl
from jax.experimental.pallas import tpu as pltpu
from jax.sharding import Mesh, PartitionSpec as P

BLK = 64
SLOTS_A = 32
SLOTS_B = 4
INNER_A = 512
INNER_B = 16
RW = 8
KW = 8
DEPTH = 8
SIDE = 4
PAIR = 2
RING = DEPTH * PAIR
LAYERS = 2
PEERS = SIDE * LAYERS
LANES = 128
SUB = 8
TAIL = 2 * SUB
ROWS = BLK * BLK // LANES
PIECE = SLOTS_B * ROWS
HALF = RW // LAYERS
INNER = RING * SIDE * INNER_B
SLOTS = RING * SLOTS_B
CAP = 8
NONE = RING * INNER_B
OVER = 2 * KW
STEP = 4
LIST = LANES * SLOTS_B + STEP

VMEM = pl.BlockSpec(memory_space=pltpu.VMEM)
SMEM = pl.BlockSpec(memory_space=pltpu.SMEM)
ANY = pl.BlockSpec(memory_space=pl.ANY)
LIMIT = pltpu.CompilerParams(vmem_limit_bytes=24 * 1024 * 1024)
SMALL = pltpu.CompilerParams(vmem_limit_bytes=8 * 1024 * 1024)


def iota(shape, axis):
    return lax.broadcasted_iota(jnp.int32, shape, axis)


def fold_block(block):
    block = block.astype(jnp.float32)
    return jnp.concatenate([block[:ROWS], block[ROWS:]], axis=1).astype(jnp.bfloat16)


def pack_kernel(b_ref, index_ref, count_ref, out_ref, piece):
    at = lax.axis_index("z") * PAIR + lax.axis_index("pair")
    row = iota((TAIL, LANES), 0)
    live = (row & (SUB - 1)) < jnp.broadcast_to(count_ref[...], (TAIL, LANES))
    codes = jnp.where(row < SUB, float(NONE), 0.0)
    for s in range(SLOTS_B):
        piece[s * ROWS : (s + 1) * ROWS, :] = fold_block(b_ref[s, 0])
        place = jnp.broadcast_to(at * INNER_B + index_ref[0, 0:1, s : s + 1], (TAIL, LANES)).astype(jnp.float32)
        column = jnp.broadcast_to(index_ref[0, 1:2, s : s + 1], (TAIL, LANES)).astype(jnp.float32)
        codes = jnp.where((row == s) & live, place, codes)
        codes = jnp.where((row == SUB + s) & live, column, codes)
    piece[PIECE:, :] = codes.astype(jnp.bfloat16)
    for peer in range(RING):
        out_ref[peer] = piece[...]


def pack_a_kernel(a_ref, index_ref, count_ref, out_ref, keys_ref, wide):
    col = lax.axis_index("col")
    wide[...] = jnp.zeros_like(wide)
    wide[0:2, 0:SLOTS_A] = index_ref[0]
    keys = wide[0:1, :] * INNER + col * INNER_A + wide[1:2, :]
    keys = jnp.where(iota((1, LANES), 1) < count_ref[...], keys, -1)
    keys = jnp.broadcast_to(keys, (SUB, LANES))
    keys = jnp.where(col == 0, keys, pltpu.roll(keys, SLOTS_A, 1))
    keys_ref[...] = keys
    for i in range(SLOTS_A):
        out_ref[i * ROWS : (i + 1) * ROWS, :] = fold_block(a_ref[0, i])
    digits = jnp.concatenate([(keys + 1) >> 6, (keys + 1) & 63], axis=0)
    out_ref[SLOTS_A * ROWS :, :] = digits.astype(jnp.float32).astype(jnp.bfloat16)


def join_kernel(own_ref, core_ref, out_ref):
    out_ref[...] = jnp.maximum(own_ref[...], core_ref[...])


def select_kernel(
    ring_ref, keys0_ref, keys1_ref, keys2_ref, keys3_ref, out_ref, codes, info_v, info_s, cnt, sem
):
    y = lax.axis_index("y")
    lane = iota((SUB, LANES), 1)
    sub = iota((SUB, LANES), 0)
    left = lane < BLK
    half = jnp.where(left, 0, 1)
    wanted, weight = [], []
    for back, keys_ref in enumerate((keys0_ref, keys1_ref, keys2_ref, keys3_ref)):
        keys = keys_ref[...]
        keys = jnp.where(left, keys, pltpu.roll(keys, BLK, 1))
        mine = (keys >= 0) & (keys >> 12 == half)
        wanted.append(jnp.where(mine, keys & (INNER - 1), -1))
        low = 1 << (3 * LAYERS * ((y + SIDE - back) & (SIDE - 1)))
        weight.append(jnp.where(left, low, low << 3))
    rows = [jnp.zeros((SUB, LANES), jnp.int32) for _ in range(3)]
    for g in range(RING):
        tail = ring_ref[g, PIECE:, :].astype(jnp.float32).astype(jnp.int32)
        place, column = tail[:SUB], tail[SUB:]
        inner = ((g >> 1 << 3) + y * PAIR + (g & 1)) * INNER_B + (place & (INNER_B - 1))
        inner = jnp.where(place < NONE, inner, -2)
        counts = jnp.zeros((SUB, LANES), jnp.int32)
        for k in range(SIDE):
            counts = counts + jnp.where(inner == wanted[k], weight[k], 0)
        total = jnp.sum(counts.astype(jnp.float32), axis=1, keepdims=True).astype(jnp.int32)
        spot = (lane == g * SLOTS_B + sub) & (sub < SLOTS_B)
        for k, value in enumerate((total, place, column)):
            rows[k] = rows[k] + jnp.where(spot, value, 0)
    for k in range(3):
        info_v[k : k + 1, :] = jnp.sum(rows[k], axis=0, keepdims=True)
    copy = pltpu.make_async_copy(info_v, info_s, sem)
    copy.start()
    none = jnp.where(iota((TAIL, LANES), 0) < SUB, float(NONE), 0.0)
    for d in range(PEERS):
        codes[d] = none
    for d in range(PEERS + 1):
        cnt[d] = 0
    copy.wait()

    def some(g, carry):
        wants = [info_s[0, g * SLOTS_B + s] for s in range(SLOTS_B)]

        @pl.when((wants[0] | wants[1] | wants[2] | wants[3]) != 0)
        def _():
            for s in range(SLOTS_B):

                @pl.when(wants[s] != 0)
                def _(s=s):
                    place = jnp.full((1, LANES), info_s[1, g * SLOTS_B + s].astype(jnp.float32), jnp.float32)
                    column = jnp.full((1, LANES), info_s[2, g * SLOTS_B + s].astype(jnp.float32), jnp.float32)
                    block = ring_ref[g, s * ROWS : (s + 1) * ROWS, :]
                    for d in range(PEERS):

                        @pl.when(((wants[s] >> (3 * d)) & 7) != 0)
                        def _(d=d):
                            p = cnt[d]
                            cnt[d] = p + 1

                            @pl.when(p < CAP)
                            def _():
                                out_ref[d, pl.ds(pl.multiple_of(p * ROWS, ROWS), ROWS), :] = block
                                codes[d, pl.ds(p, 1), :] = place
                                codes[d, pl.ds(SUB + p, 1), :] = column

                            @pl.when(p >= CAP)
                            def _():
                                cnt[PEERS] = 1

        return carry

    lax.fori_loop(0, RING, some, 0)
    over = jnp.where(iota((TAIL, LANES), 0) < SUB, 0, cnt[PEERS] * OVER).astype(jnp.float32)
    for d in range(PEERS):
        out_ref[d, CAP * ROWS :, :] = (codes[d] + over).astype(jnp.bfloat16)


def all_kernel(ring_ref, out_ref, message, sems):
    first = (iota((TAIL, LANES), 0) & (SUB - 1)) < SLOTS_B
    for g in range(RING):
        message[g * PIECE : (g + 1) * PIECE, :] = ring_ref[g, :PIECE, :]
    for chunk in range(SLOTS // SUB):
        tails = [ring_ref[2 * chunk + k, PIECE:, :].astype(jnp.float32) for k in range(2)]
        tail = jnp.where(first, tails[0], pltpu.roll(tails[1], SLOTS_B, 0))
        at = RING * PIECE + chunk * TAIL
        message[at : at + TAIL, :] = tail.astype(jnp.bfloat16)
    copies = [pltpu.make_async_copy(message, out_ref.at[d], sems.at[d]) for d in range(PEERS)]
    for copy in copies:
        copy.start()
    for copy in copies:
        copy.wait()


def spread(folded):
    wide = folded.astype(jnp.float32)
    left = iota((ROWS, LANES), 1) < BLK
    both = jnp.concatenate([jnp.where(left, wide, 0.0), jnp.where(left, 0.0, wide)], axis=0)
    return both.astype(jnp.bfloat16)


def unite_kernel(own_ref, core_ref, lay_ref, diag_ref, keys_ref, out_ref, all_keys_ref):
    col = lax.axis_index("col")
    layer = lax.axis_index("layer")
    for blocks, source, side in (
        (own_ref, layer, col),
        (core_ref, layer, 1 - col),
        (lay_ref, 1 - layer, col),
        (diag_ref, 1 - layer, 1 - col),
    ):
        at = (source * 2 + side) * SLOTS_A

        def one(i, carry, blocks=blocks, at=at):
            start = pl.multiple_of(i * ROWS, ROWS)
            out_ref[at + i] = spread(blocks[pl.ds(start, ROWS), :])
            return carry

        lax.fori_loop(0, SLOTS_A, one, 0, unroll=8)
    own = keys_ref[...]
    other = jnp.zeros((SUB, LANES), jnp.int32)
    for blocks in (lay_ref, diag_ref):
        digits = blocks[SLOTS_A * ROWS :, :].astype(jnp.float32).astype(jnp.int32)
        other = other + digits[:SUB] * BLK + digits[SUB:]
    other = other - 1
    first = jnp.where(layer == 0, own, other)
    second = jnp.where(layer == 0, other, own)
    keys = jnp.where(iota((SUB, LANES), 1) < BLK, first, pltpu.roll(second, BLK, 1))
    all_keys_ref[...] = jnp.where(keys >> 12 == layer, keys, -1)


def product_kernel(
    slots, chunks, a_ref, keys_ref, b_ref, out_ref, over_ref, acc, result, info_v, info_s, todo, over_s, sems, over_sem
):
    lane = iota((SUB, LANES), 1)
    sub = iota((SUB, LANES), 0)
    keys = keys_ref[...]
    inner = jnp.where(keys >= 0, (keys & (INNER - 1)) + (lane >> 6) * INNER, -1)
    some = jnp.zeros((SUB, LANES), jnp.int32)
    most = jnp.zeros((SUB, LANES), jnp.int32)
    for chunk in range(chunks):
        words = jnp.zeros((SUB, LANES), jnp.int32)
        for y in range(SIDE):
            for source in range(LAYERS):
                at = slots * ROWS + chunk * TAIL
                tail = b_ref[y * LAYERS + source, at : at + TAIL, :].astype(jnp.float32).astype(jnp.int32)
                most = jnp.maximum(most, tail[SUB:])
                place, column = tail[:SUB], tail[SUB:] & (KW - 1)
                piece = ((place >> 5) << 3) + y * PAIR + ((place >> 4) & 1)
                found = piece * INNER_B + (place & (INNER_B - 1)) + source * INNER
                found = jnp.where(place < NONE, found, -2)
                word = (1 << (3 * SUB + sub)) | (column << (3 * sub))
                words = words + jnp.where(found == inner, word, 0)
        some = some | words
        info_v[chunk + 2 : chunk + 3, :] = jnp.sum(words, axis=0, keepdims=True)
    some = jnp.max(jnp.where(some != 0, 1, 0), axis=0, keepdims=True)
    wide_lane = iota((LANES, LANES), 1)
    wide_sub = iota((LANES, LANES), 0)
    spread_out = jnp.where((wide_lane == wide_sub) & (some != 0), 1.0, 0.0)
    column_of = jnp.sum(spread_out, axis=1, keepdims=True)
    after = jnp.where((column_of > 0.0) & (wide_sub >= wide_lane), wide_sub, LANES)
    info_v[0:1, :] = jnp.min(after, axis=0, keepdims=True)
    info_v[1:2, :] = keys[0:1]
    info_v[2 + chunks : 3 + chunks, :] = most[0:1]
    copy = pltpu.make_async_copy(info_v, info_s, sems.at[0])
    copy.start()
    acc[...] = jnp.zeros_like(acc)
    copy.wait()

    over_s[0] = jnp.where(info_s[2 + chunks, 0] >= OVER, 1, 0)
    over_copy = pltpu.make_async_copy(over_s, over_ref, over_sem)
    over_copy.start()

    def gather(state):
        i, n = state
        key = info_s[1, i]
        sender = ((key >> 5) & (SIDE - 1)) * LAYERS + (i >> 6)

        for chunk in range(chunks):
            word = info_s[2 + chunk, i]

            def match(state, word=word, chunk=chunk):
                left, n = state
                low = left & -left
                p = jnp.where((low & 0xAA) != 0, 1, 0)
                p = p + jnp.where((low & 0xCC) != 0, 2, 0)
                p = p + jnp.where((low & 0xF0) != 0, 4, 0)
                todo[0, n] = i
                todo[1, n] = sender
                todo[2, n] = chunk * SUB + p
                todo[3, n] = (word >> (3 * p)) & (KW - 1)
                todo[4, n] = (key >> 10) & (HALF - 1)
                return left & (left - 1), n + 1

            left = (word >> (3 * SUB)) & 0xFF
            _, n = lax.while_loop(lambda state: state[0] != 0, match, (left, n))
        following = jnp.where(i + 1 < LANES, info_s[0, jnp.minimum(i + 1, LANES - 1)], LANES)
        return following, n

    _, n = lax.while_loop(lambda state: state[0] < LANES, gather, (info_s[0, 0], 0))
    for k in range(STEP - 1):
        todo[0, n + k] = 0
        todo[1, n + k] = 0
        todo[2, n + k] = 0
        todo[3, n + k] = 0
        todo[4, n + k] = HALF
    side_of = iota((BLK, LANES), 1) >> 6

    def several(step, carry):
        entries = [[todo[f, step * STEP + k] for f in range(5)] for k in range(STEP)]
        sums = []
        for block, sender, slot, column, _ in entries:
            start = pl.multiple_of(slot * ROWS, ROWS)
            b = spread(b_ref[sender, pl.ds(start, ROWS), :])
            b = jnp.concatenate([b, b], axis=0)
            terms = jnp.dot(a_ref[block], b, preferred_element_type=jnp.float32)
            terms = terms + pltpu.roll(terms, BLK, 1)
            sums.append(jnp.where(side_of == (column & 1), terms, 0.0))
        for (_, _, _, column, row), terms in zip(entries, sums):
            row = pl.multiple_of(row * BLK, BLK)
            to = pl.multiple_of((column >> 1) * LANES, LANES)
            acc[pl.ds(row, BLK), pl.ds(to, LANES)] += terms
        return carry

    lax.fori_loop(0, (n + STEP - 1) // STEP, several, 0)
    copies = []
    for r in range(HALF):
        rows = pl.ds(r * BLK, BLK)
        result[rows, :] = acc[rows, :].astype(result.dtype)
        copies.append(pltpu.make_async_copy(result.at[rows, :], out_ref.at[rows, :], sems.at[r]))
        copies[r].start()
    over_copy.wait()
    for copy in copies:
        copy.wait()


def product_call(slots, chunks, *operands):
    info = -(-(chunks + 3) // SUB) * SUB
    return pl.pallas_call(
        functools.partial(product_kernel, slots, chunks),
        out_shape=(
            jax.ShapeDtypeStruct((HALF * BLK, KW * BLK), jnp.bfloat16),
            jax.ShapeDtypeStruct((1,), jnp.int32),
        ),
        in_specs=[VMEM] * 3,
        out_specs=(ANY, ANY),
        scratch_shapes=[
            pltpu.VMEM((HALF * BLK + BLK, KW * BLK), jnp.float32),
            pltpu.VMEM((HALF * BLK, KW * BLK), jnp.bfloat16),
            pltpu.VMEM((info, LANES), jnp.int32),
            pltpu.SMEM((info, LANES), jnp.int32),
            pltpu.SMEM((5, LIST), jnp.int32),
            pltpu.SMEM((1,), jnp.int32),
            pltpu.SemaphoreType.DMA((HALF,)),
            pltpu.SemaphoreType.DMA,
        ],
        compiler_params=LIMIT,
        name=f"product_{slots}",
    )(*operands)


def on_device(a_blocks, a_index, a_count, b_blocks, b_index, b_count):
    swap = [(0, 1), (1, 0)]
    a_index = jnp.transpose(a_index, (0, 2, 1))
    b_index = jnp.transpose(b_index, (1, 2, 0))
    to_ring = pl.pallas_call(
        pack_kernel,
        out_shape=jax.ShapeDtypeStruct((RING, PIECE + TAIL, LANES), jnp.bfloat16),
        in_specs=[VMEM] * 3,
        out_specs=VMEM,
        scratch_shapes=[pltpu.VMEM((PIECE + TAIL, LANES), jnp.bfloat16)],
        name="pack",
    )(b_blocks, b_index, b_count)
    a_blocks, a_index, a_count, to_ring = lax.optimization_barrier((a_blocks, a_index, a_count, to_ring))
    a_own, keys = pl.pallas_call(
        pack_a_kernel,
        out_shape=(
            jax.ShapeDtypeStruct((SLOTS_A * ROWS + TAIL, LANES), jnp.bfloat16),
            jax.ShapeDtypeStruct((SUB, LANES), jnp.int32),
        ),
        in_specs=[VMEM] * 3,
        out_specs=(VMEM, VMEM),
        scratch_shapes=[pltpu.VMEM((SUB, LANES), jnp.int32)],
        compiler_params=SMALL,
        name="pack_a",
    )(a_blocks, a_index, a_count)
    keys_core = lax.ppermute(keys, "col", swap)
    ring = lax.all_to_all(to_ring, ("z", "pair"), 0, 0)

    joined = pl.pallas_call(
        join_kernel,
        out_shape=jax.ShapeDtypeStruct((SUB, LANES), jnp.int32),
        in_specs=[VMEM] * 2,
        out_specs=VMEM,
        compiler_params=SMALL,
        name="join_keys",
    )(keys, keys_core)
    behind = [lax.ppermute(joined, "y", [(y, (y + k) % SIDE) for y in range(SIDE)]) for k in range(1, SIDE)]
    a_core = lax.ppermute(a_own, "col", swap)
    a_layer = lax.ppermute(a_own, "layer", swap)

    to_peers = pl.pallas_call(
        select_kernel,
        out_shape=jax.ShapeDtypeStruct((PEERS, CAP * ROWS + TAIL, LANES), jnp.bfloat16),
        in_specs=[VMEM] * 5,
        out_specs=VMEM,
        scratch_shapes=[
            pltpu.VMEM((PEERS, TAIL, LANES), jnp.float32),
            pltpu.VMEM((SUB, LANES), jnp.int32),
            pltpu.SMEM((SUB, LANES), jnp.int32),
            pltpu.SMEM((PEERS + 1,), jnp.int32),
            pltpu.SemaphoreType.DMA,
        ],
        compiler_params=SMALL,
        name="select",
    )(ring, joined, *behind)
    received = lax.all_to_all(to_peers, ("y", "layer"), 0, 0)

    a_diag = lax.ppermute(a_layer, "col", swap)
    operands = pl.pallas_call(
        unite_kernel,
        out_shape=(
            jax.ShapeDtypeStruct((LANES, BLK, LANES), jnp.bfloat16),
            jax.ShapeDtypeStruct((SUB, LANES), jnp.int32),
        ),
        in_specs=[VMEM] * 5,
        out_specs=(VMEM, VMEM),
        compiler_params=SMALL,
        name="unite_a",
    )(a_own, a_core, a_layer, a_diag, joined)
    result, over = product_call(CAP, 1, *operands, received)

    def chosen(result, ring, *operands):
        return result

    def whole(result, ring, *operands):
        rows = SLOTS * ROWS + SLOTS // SUB * TAIL
        to_all = pl.pallas_call(
            all_kernel,
            out_shape=jax.ShapeDtypeStruct((PEERS, rows, LANES), jnp.bfloat16),
            in_specs=[VMEM],
            out_specs=ANY,
            scratch_shapes=[
                pltpu.VMEM((rows, LANES), jnp.bfloat16),
                pltpu.SemaphoreType.DMA((PEERS,)),
            ],
            compiler_params=LIMIT,
            name="all_blocks",
        )(ring)
        everything = lax.all_to_all(to_all, ("y", "layer"), 0, 0)
        return product_call(SLOTS, SLOTS // SUB, *operands, everything)[0]

    return lax.cond(over[0] > 0, whole, chosen, result, ring, *operands)


def solution(mesh):
    fine = Mesh(mesh.devices.reshape(DEPTH, SIDE, PAIR, 2, LAYERS), ("z", "y", "pair", "col", "layer"))
    row = ("z", "y", "pair")
    in_specs = (
        P(row, ("col", "layer"), None, None),
        P(row, ("col", "layer"), None),
        P(row, ("col", "layer")),
        P((*row, "layer"), "col", None, None),
        P((*row, "layer"), "col", None),
        P((*row, "layer"), "col"),
    )
    out_specs = P((*row, "layer"), "col")
    return jax.shard_map(
        on_device, mesh=fine, in_specs=in_specs, out_specs=out_specs, check_vma=False
    )
```

profile of v0, /device:TPU:2, one launch (start us, length us, event | category | flops | bytes accessed | tf_op | source)
XLA Modules:
  0.0 51.2 jit_solution(1334706747766730777)
XLA Ops:
  0.7 1.8 %pack.1 = bf16[16,144,128]{2,1,0:T(8,128)(2,1)} custom-call(bf16[4,1,64,64]{3,2,1,0:T(8,128)(2,1)} %b_ref.1, s32[1,2,4]{2,1,0:T(2,128)} %bitcast.4, s32[1,1]{1,0:T(1,128)S(6)} %copy.12.count_ref), custom_call_target="tpu_custom_call" | custom-call | tf_op jit(solution)/shard_map/pack/pallas_call | solution.py:351
  2.5 10.1 %all-to-all-start.1 = ((bf16[16,144,128]{2,1,0:T(8,128)(2,1)}), bf16[16,144,128]{2,1,0:T(8,128)(2,1)S(1)}, u32[]{:S(2)}, u32[]{:S(2)}) async-start(bf16[16,144,128]{2,1,0:T(8,128)(2,1)} %pack.1), calls=%async_computation.1 | async-start | bytes 1179648 | tf_op jit(solution)/shard_map/all_to_all | solution.py:373
  13.3 0.0 copy-start
  13.3 1.0 %copy-done = bf16[1,32,64,64]{3,2,1,0:T(8,128)(2,1)S(1)} copy-done((bf16[1,32,64,64]{3,2,1,0:T(8,128)(2,1)S(1)}, bf16[1,32,64,64]{3,2,1,0:T(8,128)(2,1)}, u32[]{:S(2)}) %copy-start) | copy-done | bytes 262168
  14.3 0.0 copy-start.1
  14.3 0.7 %copy-done.1 = s32[1,32,2]{1,2,0:T(2,128)S(1)} copy-done((s32[1,32,2]{1,2,0:T(2,128)S(1)}, s32[1,32,2]{1,2,0:T(2,128)}, u32[]{:S(2)}) %copy-start.1) | copy-done | bytes 280
  15.0 0.1 pack_a.1
  15.2 1.5 %collective-permute-start.1 = (bf16[1040,128]{1,0:T(8,128)(2,1)S(1)}, bf16[1040,128]{1,0:T(8,128)(2,1)S(1)}, u32[]{:S(2)}, u32[]{:S(2)}) collective-permute-start(bf16[1040,128]{1,0:T(8,128)(2,1)S(1)} %get-tuple-element.32.own_ref), channel_id=1, source_target_pairs={{0,1},{1,0},{2,3},{3,2},{4,5},{5,4},{6,7},{7,6},{8,9},{9,8},{10,11... | collective-permute-start | bytes 798728 | tf_op jit(solution)/shard_map/ppermute | solution.py:385
  16.7 0.0 collective-permute-start.3
  16.7 1.2 %collective-permute-done.3.core_ref = s32[8,128]{1,0:T(8,128)S(1)} collective-permute-done((s32[8,128]{1,0:T(8,128)S(1)}, s32[8,128]{1,0:T(8,128)S(1)}, u32[]{:S(2)}, u32[]{:S(2)}) %collective-permute-start.3) | collective-permute-done | bytes 4128 | tf_op jit(solution)/shard_map/ppermute | solution.py:372
  17.9 3.0 %collective-permute-start.6 = (s32[8,128]{1,0:T(8,128)S(1)}, s32[8,128]{1,0:T(8,128)S(1)}, u32[]{:S(2)}, u32[]{:S(2)}) collective-permute-start(s32[8,128]{1,0:T(8,128)S(1)} %join_keys.1.keys_ref.keys0_ref), channel_id=1, source_target_pairs={{0,24},{8,0},{16,8},{24,16},{1,25},{9,1},{17,9},{25,17},{2,26},{10... | collective-permute-start | bytes 12296 | tf_op jit(solution)/shard_map/ppermute | solution.py:383
  20.9 0.6 %collective-permute-start.5 = (s32[8,128]{1,0:T(8,128)S(1)}, s32[8,128]{1,0:T(8,128)S(1)}, u32[]{:S(2)}, u32[]{:S(2)}) collective-permute-start(s32[8,128]{1,0:T(8,128)S(1)} %join_keys.1.keys_ref.keys0_ref), channel_id=1, source_target_pairs={{0,16},{8,24},{16,0},{24,8},{1,17},{9,25},{17,1},{25,9},{2,18},{10... | collective-permute-start | bytes 12296 | tf_op jit(solution)/shard_map/ppermute | solution.py:383
  21.5 1.0 %collective-permute-start.4 = (s32[8,128]{1,0:T(8,128)S(1)}, s32[8,128]{1,0:T(8,128)S(1)}, u32[]{:S(2)}, u32[]{:S(2)}) collective-permute-start(s32[8,128]{1,0:T(8,128)S(1)} %join_keys.1.keys_ref.keys0_ref), channel_id=1, source_target_pairs={{0,8},{8,16},{16,24},{24,0},{1,9},{9,17},{17,25},{25,1},{2,10},{10... | collective-permute-start | bytes 12296 | tf_op jit(solution)/shard_map/ppermute | solution.py:383
  22.5 0.0 collective-permute-done.6.keys3_ref
  22.5 3.5 %collective-permute-done.5.keys2_ref = s32[8,128]{1,0:T(8,128)S(1)} collective-permute-done((s32[8,128]{1,0:T(8,128)S(1)}, s32[8,128]{1,0:T(8,128)S(1)}, u32[]{:S(2)}, u32[]{:S(2)}) %collective-permute-start.5) | collective-permute-done | bytes 4128 | tf_op jit(solution)/shard_map/ppermute | solution.py:383
  26.0 0.3 collective-permute-done.4.keys1_ref
  26.3 6.6 %all-to-all-done.1.ring_ref = bf16[16,144,128]{2,1,0:T(8,128)(2,1)S(1)} async-done(((bf16[16,144,128]{2,1,0:T(8,128)(2,1)}), bf16[16,144,128]{2,1,0:T(8,128)(2,1)S(1)}, u32[]{:S(2)}, u32[]{:S(2)}) %all-to-all-start.1) | async-done | bytes 589856 | tf_op jit(solution)/shard_map/all_to_all | solution.py:373
  32.9 0.0 copy-start.2
  32.9 2.2 %select.1 = bf16[8,272,128]{2,1,0:T(8,128)(2,1)} custom-call(bf16[16,144,128]{2,1,0:T(8,128)(2,1)S(1)} %all-to-all-done.1.ring_ref, s32[8,128]{1,0:T(8,128)S(1)} %join_keys.1.keys_ref.keys0_ref, s32[8,128]{1,0:T(8,128)S(1)} %collective-permute-done.4.keys1_ref, s32[8,128]{1,0:T(8,128)S(1)} %collective-permute-done.5.keys2_ref, ...), custom_call_target="tpu_custom_call" | custom-call | tf_op jit(solution)/shard_map/select/pallas_call | solution.py:387
  35.1 6.0 %all-to-all-start.2 = ((bf16[8,272,128]{2,1,0:T(8,128)(2,1)}), bf16[8,272,128]{2,1,0:T(8,128)(2,1)S(1)}, u32[]{:S(2)}, u32[]{:S(2)}) async-start(bf16[8,272,128]{2,1,0:T(8,128)(2,1)} %select.1), calls=%async_computation.2 | async-start | bytes 1114112 | tf_op jit(solution)/shard_map/all_to_all | solution.py:402
  41.1 0.0 collective-permute-start
  41.1 0.0 collective-permute-done.1.lay_ref
  41.1 0.5 collective-permute-start.2
  41.6 1.0 %collective-permute-done.core_ref = bf16[1040,128]{1,0:T(8,128)(2,1)S(1)} collective-permute-done((bf16[1040,128]{1,0:T(8,128)(2,1)S(1)}, bf16[1040,128]{1,0:T(8,128)(2,1)S(1)}, u32[]{:S(2)}, u32[]{:S(2)}) %collective-permute-start) | collective-permute-done | bytes 266272 | tf_op jit(solution)/shard_map/ppermute | solution.py:384
  42.6 0.0 copy-done.2
  42.6 0.4 collective-permute-done.2.diag_ref
  43.0 0.4 unite_a.1
  43.4 5.3 %all-to-all-done.2.b_ref = bf16[8,272,128]{2,1,0:T(8,128)(2,1)S(1)} async-done(((bf16[8,272,128]{2,1,0:T(8,128)(2,1)}), bf16[8,272,128]{2,1,0:T(8,128)(2,1)S(1)}, u32[]{:S(2)}, u32[]{:S(2)}) %all-to-all-start.2) | async-done | bytes 557088 | tf_op jit(solution)/shard_map/all_to_all | solution.py:402
  48.8 1.9 %product_8.1 = (bf16[256,512]{1,0:T(8,128)(2,1)}, s32[1]{0:T(128)}) custom-call(bf16[128,64,128]{2,1,0:T(8,128)(2,1)S(1)} %get-tuple-element.34.a_ref, s32[8,128]{1,0:T(8,128)S(1)} %get-tuple-element.35.keys_ref, bf16[8,272,128]{2,1,0:T(8,128)(2,1)S(1)} %all-to-all-done.2.b_ref), custom_call_target="tpu_custom_call" | custom-call | tf_op jit(solution)/shard_map/product_8/pallas_call | solution.py:324
  (2 shorter events, 0.0 us)
Async XLA Ops:
  2.5 30.4 %all-to-all-start.1 = ((bf16[16,144,128]{2,1,0:T(8,128)(2,1)}), bf16[16,144,128]{2,1,0:T(8,128)(2,1)S(1)}, u32[]{:S(2)}, u32[]{:S(2)}) async-start(bf16[16,144,128]{2,1,0:T(8,128)(2,1)} %pack.1), calls=%async_computation.1 | async-start | bytes 1179648 | tf_op jit(solution)/shard_map/all_to_all | solution.py:373
  13.3 1.0 %copy-start = (bf16[1,32,64,64]{3,2,1,0:T(8,128)(2,1)S(1)}, bf16[1,32,64,64]{3,2,1,0:T(8,128)(2,1)}, u32[]{:S(2)}) copy-start(bf16[1,32,64,64]{3,2,1,0:T(8,128)(2,1)} %a_ref) | copy-start | bytes 786436
  14.3 0.7 %copy-start.1 = (s32[1,32,2]{1,2,0:T(2,128)S(1)}, s32[1,32,2]{1,2,0:T(2,128)}, u32[]{:S(2)}) copy-start(s32[1,32,2]{1,2,0:T(2,128)} %param.9) | copy-start | bytes 772
  15.2 25.9 %collective-permute-start.1 = (bf16[1040,128]{1,0:T(8,128)(2,1)S(1)}, bf16[1040,128]{1,0:T(8,128)(2,1)S(1)}, u32[]{:S(2)}, u32[]{:S(2)}) collective-permute-start(bf16[1040,128]{1,0:T(8,128)(2,1)S(1)} %get-tuple-element.32.own_ref), channel_id=1, source_target_pairs={{0,1},{1,0},{2,3},{3,2},{4,5},{5,4},{6,7},{7,6},{8,9},{9,8},{10,11... | collective-permute-start | bytes 798728 | tf_op jit(solution)/shard_map/ppermute | solution.py:385
  16.7 1.2 %collective-permute-start.3 = (s32[8,128]{1,0:T(8,128)S(1)}, s32[8,128]{1,0:T(8,128)S(1)}, u32[]{:S(2)}, u32[]{:S(2)}) collective-permute-start(s32[8,128]{1,0:T(8,128)S(1)} %get-tuple-element.33.own_ref), channel_id=1, source_target_pairs={{0,2},{2,0},{1,3},{3,1},{4,6},{6,4},{5,7},{7,5},{8,10},{10,8},{9,1... | collective-permute-start | bytes 12296 | tf_op jit(solution)/shard_map/ppermute | solution.py:372
  17.9 4.6 %collective-permute-start.6 = (s32[8,128]{1,0:T(8,128)S(1)}, s32[8,128]{1,0:T(8,128)S(1)}, u32[]{:S(2)}, u32[]{:S(2)}) collective-permute-start(s32[8,128]{1,0:T(8,128)S(1)} %join_keys.1.keys_ref.keys0_ref), channel_id=1, source_target_pairs={{0,24},{8,0},{16,8},{24,16},{1,25},{9,1},{17,9},{25,17},{2,26},{10... | collective-permute-start | bytes 12296 | tf_op jit(solution)/shard_map/ppermute | solution.py:383
  20.9 5.1 %collective-permute-start.5 = (s32[8,128]{1,0:T(8,128)S(1)}, s32[8,128]{1,0:T(8,128)S(1)}, u32[]{:S(2)}, u32[]{:S(2)}) collective-permute-start(s32[8,128]{1,0:T(8,128)S(1)} %join_keys.1.keys_ref.keys0_ref), channel_id=1, source_target_pairs={{0,16},{8,24},{16,0},{24,8},{1,17},{9,25},{17,1},{25,9},{2,18},{10... | collective-permute-start | bytes 12296 | tf_op jit(solution)/shard_map/ppermute | solution.py:383
  21.5 4.8 %collective-permute-start.4 = (s32[8,128]{1,0:T(8,128)S(1)}, s32[8,128]{1,0:T(8,128)S(1)}, u32[]{:S(2)}, u32[]{:S(2)}) collective-permute-start(s32[8,128]{1,0:T(8,128)S(1)} %join_keys.1.keys_ref.keys0_ref), channel_id=1, source_target_pairs={{0,8},{8,16},{16,24},{24,0},{1,9},{9,17},{17,25},{25,1},{2,10},{10... | collective-permute-start | bytes 12296 | tf_op jit(solution)/shard_map/ppermute | solution.py:383
  32.9 9.7 %copy-start.2 = (bf16[16,144,128]{2,1,0:T(8,128)(2,1)}, bf16[16,144,128]{2,1,0:T(8,128)(2,1)S(1)}, u32[]{:S(2)}) copy-start(bf16[16,144,128]{2,1,0:T(8,128)(2,1)S(1)} %all-to-all-done.1.ring_ref) | copy-start | bytes 1769476
  35.1 13.7 %all-to-all-start.2 = ((bf16[8,272,128]{2,1,0:T(8,128)(2,1)}), bf16[8,272,128]{2,1,0:T(8,128)(2,1)S(1)}, u32[]{:S(2)}, u32[]{:S(2)}) async-start(bf16[8,272,128]{2,1,0:T(8,128)(2,1)} %select.1), calls=%async_computation.2 | async-start | bytes 1114112 | tf_op jit(solution)/shard_map/all_to_all | solution.py:402
  41.1 1.5 %collective-permute-start = (bf16[1040,128]{1,0:T(8,128)(2,1)S(1)}, bf16[1040,128]{1,0:T(8,128)(2,1)S(1)}, u32[]{:S(2)}, u32[]{:S(2)}) collective-permute-start(bf16[1040,128]{1,0:T(8,128)(2,1)S(1)} %get-tuple-element.32.own_ref), channel_id=1, source_target_pairs={{0,2},{2,0},{1,3},{3,1},{4,6},{6,4},{5,7},{7,5},{8,10},{10,8},{9,1... | collective-permute-start | bytes 798728 | tf_op jit(solution)/shard_map/ppermute | solution.py:384
  41.1 1.9 %collective-permute-start.2 = (bf16[1040,128]{1,0:T(8,128)(2,1)S(1)}, bf16[1040,128]{1,0:T(8,128)(2,1)S(1)}, u32[]{:S(2)}, u32[]{:S(2)}) collective-permute-start(bf16[1040,128]{1,0:T(8,128)(2,1)S(1)} %collective-permute-done.1.lay_ref), channel_id=1, source_target_pairs={{0,2},{2,0},{1,3},{3,1},{4,6},{6,4},{5,7},{7,5},{8,10},{10,8},{9,1... | collective-permute-start | bytes 798728 | tf_op jit(solution)/shard_map/ppermute | solution.py:404
where the time goes:
time: 51.9 us; the launch traced here: 51.2 us
  starting transfers between devices  22.8 us (44%)
  waiting for transfers between devices  18.4 us (35%)
  Pallas kernels  6.44 us (12%)
  between operations  1.96 us (4%)
  local copies, waits for them, and re-layouts  1.72 us (3%)
    all_to_all x1, starting transfers between devices, on_device(): ring = lax.all_to_all(to_ring, ('z', 'pair'), 0, 0)  10.1 us
    all_to_all x1, waiting for transfers between devices, on_device(): ring = lax.all_to_all(to_ring, ('z', 'pair'), 0, 0)  6.59 us
    all_to_all x1, starting transfers between devices, on_device(): received = lax.all_to_all(to_peers, ('y', 'layer'), 0, 0)  5.98 us
    all_to_all x1, waiting for transfers between devices, on_device(): received = lax.all_to_all(to_peers, ('y', 'layer'), 0, 0)  5.35 us
    ppermute x3, starting transfers between devices, on_device(): lax.ppermute(joined, 'y', [(y, (y + k) % SIDE) for y in range(SIDE)])  4.61 us
    ppermute x3, waiting for transfers between devices, on_device(): lax.ppermute(joined, 'y', [(y, (y + k) % SIDE) for y in range(SIDE)])  3.85 us
    pallas_call x1, Pallas kernels, on_device(): pl.pallas_call(select_kernel, out_shape=jax.ShapeDtypeStruct((PEERS, CAP...  2.16 us
    pallas_call x1, Pallas kernels, product_call(): pl.pallas_call(functools.partial(product_kernel, slots, chunks), out_shap...  1.85 us
  transfers between devices with their start and end apart: 9, of which 7 were waited for; matrix products, arithmetic and copies ran while one was open for 0% of the time, Pallas kernels for 5%

commit v1 on v0

--- a/solution.py
+++ b/solution.py
@@ -52,15 +52,15 @@
 
 def pack_kernel(b_ref, index_ref, count_ref, out_ref, piece):
     at = lax.axis_index("z") * PAIR + lax.axis_index("pair")
-    row = iota((TAIL, LANES), 0)
-    live = (row & (SUB - 1)) < jnp.broadcast_to(count_ref[...], (TAIL, LANES))
-    codes = jnp.where(row < SUB, float(NONE), 0.0)
+    row = iota((SUB, LANES), 0)
+    live = (row & (SLOTS_B - 1)) < jnp.broadcast_to(count_ref[...], (SUB, LANES))
+    codes = jnp.where(row < SLOTS_B, float(NONE), 0.0)
     for s in range(SLOTS_B):
         piece[s * ROWS : (s + 1) * ROWS, :] = fold_block(b_ref[s, 0])
-        place = jnp.broadcast_to(at * INNER_B + index_ref[0, 0:1, s : s + 1], (TAIL, LANES)).astype(jnp.float32)
-        column = jnp.broadcast_to(index_ref[0, 1:2, s : s + 1], (TAIL, LANES)).astype(jnp.float32)
+        place = jnp.broadcast_to(at * INNER_B + index_ref[0, 0:1, s : s + 1], (SUB, LANES)).astype(jnp.float32)
+        column = jnp.broadcast_to(index_ref[0, 1:2, s : s + 1], (SUB, LANES)).astype(jnp.float32)
         codes = jnp.where((row == s) & live, place, codes)
-        codes = jnp.where((row == SUB + s) & live, column, codes)
+        codes = jnp.where((row == SLOTS_B + s) & live, column, codes)
     piece[PIECE:, :] = codes.astype(jnp.bfloat16)
     for peer in range(RING):
         out_ref[peer] = piece[...]
@@ -103,10 +103,10 @@
         weight.append(jnp.where(left, low, low << 3))
     rows = [jnp.zeros((SUB, LANES), jnp.int32) for _ in range(3)]
     for g in range(RING):
-        tail = ring_ref[g, PIECE:, :].astype(jnp.float32).astype(jnp.int32)
-        place, column = tail[:SUB], tail[SUB:]
+        place = ring_ref[g, PIECE:, :].astype(jnp.float32).astype(jnp.int32)
+        column = pltpu.roll(place, SLOTS_B, 0)
         inner = ((g >> 1 << 3) + y * PAIR + (g & 1)) * INNER_B + (place & (INNER_B - 1))
-        inner = jnp.where(place < NONE, inner, -2)
+        inner = jnp.where((place < NONE) & (sub < SLOTS_B), inner, -2)
         counts = jnp.zeros((SUB, LANES), jnp.int32)
         for k in range(SIDE):
             counts = counts + jnp.where(inner == wanted[k], weight[k], 0)
@@ -163,14 +163,15 @@
 
 
 def all_kernel(ring_ref, out_ref, message, sems):
-    first = (iota((TAIL, LANES), 0) & (SUB - 1)) < SLOTS_B
+    first = iota((SUB, LANES), 0) < SLOTS_B
     for g in range(RING):
         message[g * PIECE : (g + 1) * PIECE, :] = ring_ref[g, :PIECE, :]
     for chunk in range(SLOTS // SUB):
         tails = [ring_ref[2 * chunk + k, PIECE:, :].astype(jnp.float32) for k in range(2)]
-        tail = jnp.where(first, tails[0], pltpu.roll(tails[1], SLOTS_B, 0))
+        places = jnp.where(first, tails[0], pltpu.roll(tails[1], SLOTS_B, 0))
+        columns = jnp.where(first, pltpu.roll(tails[0], SLOTS_B, 0), tails[1])
         at = RING * PIECE + chunk * TAIL
-        message[at : at + TAIL, :] = tail.astype(jnp.bfloat16)
+        message[at : at + TAIL, :] = jnp.concatenate([places, columns], axis=0).astype(jnp.bfloat16)
     copies = [pltpu.make_async_copy(message, out_ref.at[d], sems.at[d]) for d in range(PEERS)]
     for copy in copies:
         copy.start()
@@ -350,10 +351,10 @@
     b_index = jnp.transpose(b_index, (1, 2, 0))
     to_ring = pl.pallas_call(
         pack_kernel,
-        out_shape=jax.ShapeDtypeStruct((RING, PIECE + TAIL, LANES), jnp.bfloat16),
+        out_shape=jax.ShapeDtypeStruct((RING, PIECE + SUB, LANES), jnp.bfloat16),
         in_specs=[VMEM] * 3,
         out_specs=VMEM,
-        scratch_shapes=[pltpu.VMEM((PIECE + TAIL, LANES), jnp.bfloat16)],
+        scratch_shapes=[pltpu.VMEM((PIECE + SUB, LANES), jnp.bfloat16)],
         name="pack",
     )(b_blocks, b_index, b_count)
     a_blocks, a_index, a_count, to_ring = lax.optimization_barrier((a_blocks, a_index, a_count, to_ring))

time: 51.9 us -> 51.3 us (0.988)
  waiting for transfers between devices: 18.4 us -> 17.5 us
    all_to_all x1, waiting for transfers between devices: 6.59 us -> 5.78 us  [on_device(): ring = lax.all_to_all(to_ring, ('z', 'pair'), 0, 0)]
where the time goes in v1:
time: 51.3 us; the launch traced here: 51.1 us
  starting transfers between devices  23 us (45%)
  waiting for transfers between devices  17.5 us (34%)
  Pallas kernels  6.87 us (13%)
  between operations  1.91 us (4%)
  local copies, waits for them, and re-layouts  1.72 us (3%)
    all_to_all x1, starting transfers between devices, on_device(): ring = lax.all_to_all(to_ring, ('z', 'pair'), 0, 0)  10.1 us
    all_to_all x1, starting transfers between devices, on_device(): received = lax.all_to_all(to_peers, ('y', 'layer'), 0, 0)  6.23 us
    all_to_all x1, waiting for transfers between devices, on_device(): ring = lax.all_to_all(to_ring, ('z', 'pair'), 0, 0)  5.78 us
    all_to_all x1, waiting for transfers between devices, on_device(): received = lax.all_to_all(to_peers, ('y', 'layer'), 0, 0)  5.35 us
    ppermute x3, starting transfers between devices, on_device(): lax.ppermute(joined, 'y', [(y, (y + k) % SIDE) for y in range(SIDE)])  4.61 us
    ppermute x3, waiting for transfers between devices, on_device(): lax.ppermute(joined, 'y', [(y, (y + k) % SIDE) for y in range(SIDE)])  3.85 us
    pallas_call x1, Pallas kernels, product_call(): pl.pallas_call(functools.partial(product_kernel, slots, chunks), out_shap...  2.23 us
    pallas_call x1, Pallas kernels, on_device(): pl.pallas_call(select_kernel, out_shape=jax.ShapeDtypeStruct((PEERS, CAP...  2.22 us
  transfers between devices with their start and end apart: 9, of which 7 were waited for; matrix products, arithmetic and copies ran while one was open for 0% of the time, Pallas kernels for 5%

profile of v1, /device:TPU:2, one launch (start us, length us, event | category | flops | bytes accessed | tf_op | source)
XLA Modules:
  0.0 51.1 jit_solution(12453143010808973062)
XLA Ops:
  0.7 1.8 %pack.1 = bf16[16,136,128]{2,1,0:T(8,128)(2,1)} custom-call(bf16[4,1,64,64]{3,2,1,0:T(8,128)(2,1)} %b_ref.1, s32[1,2,4]{2,1,0:T(2,128)} %bitcast.4, s32[1,1]{1,0:T(1,128)S(6)} %copy.12.count_ref), custom_call_target="tpu_custom_call" | custom-call | tf_op jit(solution)/shard_map/pack/pallas_call | solution.py:352
  2.5 10.1 %all-to-all-start.1 = ((bf16[16,136,128]{2,1,0:T(8,128)(2,1)}), bf16[16,136,128]{2,1,0:T(8,128)(2,1)S(1)}, u32[]{:S(2)}, u32[]{:S(2)}) async-start(bf16[16,136,128]{2,1,0:T(8,128)(2,1)} %pack.1), calls=%async_computation.1 | async-start | bytes 1114112 | tf_op jit(solution)/shard_map/all_to_all | solution.py:374
  13.3 0.0 copy-start
  13.3 1.0 %copy-done = bf16[1,32,64,64]{3,2,1,0:T(8,128)(2,1)S(1)} copy-done((bf16[1,32,64,64]{3,2,1,0:T(8,128)(2,1)S(1)}, bf16[1,32,64,64]{3,2,1,0:T(8,128)(2,1)}, u32[]{:S(2)}) %copy-start) | copy-done | bytes 262168
  14.3 0.0 copy-start.1
  14.3 0.7 %copy-done.1 = s32[1,32,2]{1,2,0:T(2,128)S(1)} copy-done((s32[1,32,2]{1,2,0:T(2,128)S(1)}, s32[1,32,2]{1,2,0:T(2,128)}, u32[]{:S(2)}) %copy-start.1) | copy-done | bytes 280
  15.0 0.1 pack_a.1
  15.2 1.5 %collective-permute-start.1 = (bf16[1040,128]{1,0:T(8,128)(2,1)S(1)}, bf16[1040,128]{1,0:T(8,128)(2,1)S(1)}, u32[]{:S(2)}, u32[]{:S(2)}) collective-permute-start(bf16[1040,128]{1,0:T(8,128)(2,1)S(1)} %get-tuple-element.32.own_ref), channel_id=1, source_target_pairs={{0,1},{1,0},{2,3},{3,2},{4,5},{5,4},{6,7},{7,6},{8,9},{9,8},{10,11... | collective-permute-start | bytes 798728 | tf_op jit(solution)/shard_map/ppermute | solution.py:386
  16.7 0.0 collective-permute-start.3
  16.7 1.2 %collective-permute-done.3.core_ref = s32[8,128]{1,0:T(8,128)S(1)} collective-permute-done((s32[8,128]{1,0:T(8,128)S(1)}, s32[8,128]{1,0:T(8,128)S(1)}, u32[]{:S(2)}, u32[]{:S(2)}) %collective-permute-start.3) | collective-permute-done | bytes 4128 | tf_op jit(solution)/shard_map/ppermute | solution.py:373
  17.8 3.0 %collective-permute-start.6 = (s32[8,128]{1,0:T(8,128)S(1)}, s32[8,128]{1,0:T(8,128)S(1)}, u32[]{:S(2)}, u32[]{:S(2)}) collective-permute-start(s32[8,128]{1,0:T(8,128)S(1)} %join_keys.1.keys_ref.keys0_ref), channel_id=1, source_target_pairs={{0,24},{8,0},{16,8},{24,16},{1,25},{9,1},{17,9},{25,17},{2,26},{10... | collective-permute-start | bytes 12296 | tf_op jit(solution)/shard_map/ppermute | solution.py:384
  20.9 0.6 %collective-permute-start.5 = (s32[8,128]{1,0:T(8,128)S(1)}, s32[8,128]{1,0:T(8,128)S(1)}, u32[]{:S(2)}, u32[]{:S(2)}) collective-permute-start(s32[8,128]{1,0:T(8,128)S(1)} %join_keys.1.keys_ref.keys0_ref), channel_id=1, source_target_pairs={{0,16},{8,24},{16,0},{24,8},{1,17},{9,25},{17,1},{25,9},{2,18},{10... | collective-permute-start | bytes 12296 | tf_op jit(solution)/shard_map/ppermute | solution.py:384
  21.5 1.0 %collective-permute-start.4 = (s32[8,128]{1,0:T(8,128)S(1)}, s32[8,128]{1,0:T(8,128)S(1)}, u32[]{:S(2)}, u32[]{:S(2)}) collective-permute-start(s32[8,128]{1,0:T(8,128)S(1)} %join_keys.1.keys_ref.keys0_ref), channel_id=1, source_target_pairs={{0,8},{8,16},{16,24},{24,0},{1,9},{9,17},{17,25},{25,1},{2,10},{10... | collective-permute-start | bytes 12296 | tf_op jit(solution)/shard_map/ppermute | solution.py:384
  22.5 0.0 collective-permute-done.6.keys3_ref
  22.5 3.5 %collective-permute-done.5.keys2_ref = s32[8,128]{1,0:T(8,128)S(1)} collective-permute-done((s32[8,128]{1,0:T(8,128)S(1)}, s32[8,128]{1,0:T(8,128)S(1)}, u32[]{:S(2)}, u32[]{:S(2)}) %collective-permute-start.5) | collective-permute-done | bytes 4128 | tf_op jit(solution)/shard_map/ppermute | solution.py:384
  26.0 0.3 collective-permute-done.4.keys1_ref
  26.3 5.8 %all-to-all-done.1.ring_ref = bf16[16,136,128]{2,1,0:T(8,128)(2,1)S(1)} async-done(((bf16[16,136,128]{2,1,0:T(8,128)(2,1)}), bf16[16,136,128]{2,1,0:T(8,128)(2,1)S(1)}, u32[]{:S(2)}, u32[]{:S(2)}) %all-to-all-start.1) | async-done | bytes 557088 | tf_op jit(solution)/shard_map/all_to_all | solution.py:374
  32.1 0.0 copy-start.2
  32.1 2.2 %select.1 = bf16[8,272,128]{2,1,0:T(8,128)(2,1)} custom-call(bf16[16,136,128]{2,1,0:T(8,128)(2,1)S(1)} %all-to-all-done.1.ring_ref, s32[8,128]{1,0:T(8,128)S(1)} %join_keys.1.keys_ref.keys0_ref, s32[8,128]{1,0:T(8,128)S(1)} %collective-permute-done.4.keys1_ref, s32[8,128]{1,0:T(8,128)S(1)} %collective-permute-done.5.keys2_ref, ...), custom_call_target="tpu_custom_call" | custom-call | tf_op jit(solution)/shard_map/select/pallas_call | solution.py:388
  34.3 6.2 %all-to-all-start.2 = ((bf16[8,272,128]{2,1,0:T(8,128)(2,1)}), bf16[8,272,128]{2,1,0:T(8,128)(2,1)S(1)}, u32[]{:S(2)}, u32[]{:S(2)}) async-start(bf16[8,272,128]{2,1,0:T(8,128)(2,1)} %select.1), calls=%async_computation.2 | async-start | bytes 1114112 | tf_op jit(solution)/shard_map/all_to_all | solution.py:403
  40.6 0.0 collective-permute-start
  40.6 0.0 collective-permute-done.1.lay_ref
  40.6 0.5 collective-permute-start.2
  41.1 1.0 %collective-permute-done.core_ref = bf16[1040,128]{1,0:T(8,128)(2,1)S(1)} collective-permute-done((bf16[1040,128]{1,0:T(8,128)(2,1)S(1)}, bf16[1040,128]{1,0:T(8,128)(2,1)S(1)}, u32[]{:S(2)}, u32[]{:S(2)}) %collective-permute-start) | collective-permute-done | bytes 266272 | tf_op jit(solution)/shard_map/ppermute | solution.py:385
  42.1 0.0 copy-done.2
  42.1 0.4 collective-permute-done.2.diag_ref
  42.5 0.4 unite_a.1
  42.9 5.3 %all-to-all-done.2.b_ref = bf16[8,272,128]{2,1,0:T(8,128)(2,1)S(1)} async-done(((bf16[8,272,128]{2,1,0:T(8,128)(2,1)}), bf16[8,272,128]{2,1,0:T(8,128)(2,1)S(1)}, u32[]{:S(2)}, u32[]{:S(2)}) %all-to-all-start.2) | async-done | bytes 557088 | tf_op jit(solution)/shard_map/all_to_all | solution.py:403
  48.3 2.2 %product_8.1 = (bf16[256,512]{1,0:T(8,128)(2,1)}, s32[1]{0:T(128)}) custom-call(bf16[128,64,128]{2,1,0:T(8,128)(2,1)S(1)} %get-tuple-element.34.a_ref, s32[8,128]{1,0:T(8,128)S(1)} %get-tuple-element.35.keys_ref, bf16[8,272,128]{2,1,0:T(8,128)(2,1)S(1)} %all-to-all-done.2.b_ref), custom_call_target="tpu_custom_call" | custom-call | tf_op jit(solution)/shard_map/product_8/pallas_call | solution.py:325
  (2 shorter events, 0.0 us)
Async XLA Ops:
  2.5 29.6 %all-to-all-start.1 = ((bf16[16,136,128]{2,1,0:T(8,128)(2,1)}), bf16[16,136,128]{2,1,0:T(8,128)(2,1)S(1)}, u32[]{:S(2)}, u32[]{:S(2)}) async-start(bf16[16,136,128]{2,1,0:T(8,128)(2,1)} %pack.1), calls=%async_computation.1 | async-start | bytes 1114112 | tf_op jit(solution)/shard_map/all_to_all | solution.py:374
  13.3 1.0 %copy-start = (bf16[1,32,64,64]{3,2,1,0:T(8,128)(2,1)S(1)}, bf16[1,32,64,64]{3,2,1,0:T(8,128)(2,1)}, u32[]{:S(2)}) copy-start(bf16[1,32,64,64]{3,2,1,0:T(8,128)(2,1)} %a_ref) | copy-start | bytes 786436
  14.3 0.7 %copy-start.1 = (s32[1,32,2]{1,2,0:T(2,128)S(1)}, s32[1,32,2]{1,2,0:T(2,128)}, u32[]{:S(2)}) copy-start(s32[1,32,2]{1,2,0:T(2,128)} %param.9) | copy-start | bytes 772
  15.2 25.4 %collective-permute-start.1 = (bf16[1040,128]{1,0:T(8,128)(2,1)S(1)}, bf16[1040,128]{1,0:T(8,128)(2,1)S(1)}, u32[]{:S(2)}, u32[]{:S(2)}) collective-permute-start(bf16[1040,128]{1,0:T(8,128)(2,1)S(1)} %get-tuple-element.32.own_ref), channel_id=1, source_target_pairs={{0,1},{1,0},{2,3},{3,2},{4,5},{5,4},{6,7},{7,6},{8,9},{9,8},{10,11... | collective-permute-start | bytes 798728 | tf_op jit(solution)/shard_map/ppermute | solution.py:386
  16.7 1.2 %collective-permute-start.3 = (s32[8,128]{1,0:T(8,128)S(1)}, s32[8,128]{1,0:T(8,128)S(1)}, u32[]{:S(2)}, u32[]{:S(2)}) collective-permute-start(s32[8,128]{1,0:T(8,128)S(1)} %get-tuple-element.33.own_ref), channel_id=1, source_target_pairs={{0,2},{2,0},{1,3},{3,1},{4,6},{6,4},{5,7},{7,5},{8,10},{10,8},{9,1... | collective-permute-start | bytes 12296 | tf_op jit(solution)/shard_map/ppermute | solution.py:373
  17.8 4.6 %collective-permute-start.6 = (s32[8,128]{1,0:T(8,128)S(1)}, s32[8,128]{1,0:T(8,128)S(1)}, u32[]{:S(2)}, u32[]{:S(2)}) collective-permute-start(s32[8,128]{1,0:T(8,128)S(1)} %join_keys.1.keys_ref.keys0_ref), channel_id=1, source_target_pairs={{0,24},{8,0},{16,8},{24,16},{1,25},{9,1},{17,9},{25,17},{2,26},{10... | collective-permute-start | bytes 12296 | tf_op jit(solution)/shard_map/ppermute | solution.py:384
  20.9 5.1 %collective-permute-start.5 = (s32[8,128]{1,0:T(8,128)S(1)}, s32[8,128]{1,0:T(8,128)S(1)}, u32[]{:S(2)}, u32[]{:S(2)}) collective-permute-start(s32[8,128]{1,0:T(8,128)S(1)} %join_keys.1.keys_ref.keys0_ref), channel_id=1, source_target_pairs={{0,16},{8,24},{16,0},{24,8},{1,17},{9,25},{17,1},{25,9},{2,18},{10... | collective-permute-start | bytes 12296 | tf_op jit(solution)/shard_map/ppermute | solution.py:384
  21.5 4.8 %collective-permute-start.4 = (s32[8,128]{1,0:T(8,128)S(1)}, s32[8,128]{1,0:T(8,128)S(1)}, u32[]{:S(2)}, u32[]{:S(2)}) collective-permute-start(s32[8,128]{1,0:T(8,128)S(1)} %join_keys.1.keys_ref.keys0_ref), channel_id=1, source_target_pairs={{0,8},{8,16},{16,24},{24,0},{1,9},{9,17},{17,25},{25,1},{2,10},{10... | collective-permute-start | bytes 12296 | tf_op jit(solution)/shard_map/ppermute | solution.py:384
  32.1 10.0 %copy-start.2 = (bf16[16,136,128]{2,1,0:T(8,128)(2,1)}, bf16[16,136,128]{2,1,0:T(8,128)(2,1)S(1)}, u32[]{:S(2)}) copy-start(bf16[16,136,128]{2,1,0:T(8,128)(2,1)S(1)} %all-to-all-done.1.ring_ref) | copy-start | bytes 1671172
  34.3 13.9 %all-to-all-start.2 = ((bf16[8,272,128]{2,1,0:T(8,128)(2,1)}), bf16[8,272,128]{2,1,0:T(8,128)(2,1)S(1)}, u32[]{:S(2)}, u32[]{:S(2)}) async-start(bf16[8,272,128]{2,1,0:T(8,128)(2,1)} %select.1), calls=%async_computation.2 | async-start | bytes 1114112 | tf_op jit(solution)/shard_map/all_to_all | solution.py:403
  40.6 1.5 %collective-permute-start = (bf16[1040,128]{1,0:T(8,128)(2,1)S(1)}, bf16[1040,128]{1,0:T(8,128)(2,1)S(1)}, u32[]{:S(2)}, u32[]{:S(2)}) collective-permute-start(bf16[1040,128]{1,0:T(8,128)(2,1)S(1)} %get-tuple-element.32.own_ref), channel_id=1, source_target_pairs={{0,2},{2,0},{1,3},{3,1},{4,6},{6,4},{5,7},{7,5},{8,10},{10,8},{9,1... | collective-permute-start | bytes 798728 | tf_op jit(solution)/shard_map/ppermute | solution.py:385
  40.6 1.9 %collective-permute-start.2 = (bf16[1040,128]{1,0:T(8,128)(2,1)S(1)}, bf16[1040,128]{1,0:T(8,128)(2,1)S(1)}, u32[]{:S(2)}, u32[]{:S(2)}) collective-permute-start(bf16[1040,128]{1,0:T(8,128)(2,1)S(1)} %collective-permute-done.1.lay_ref), channel_id=1, source_target_pairs={{0,2},{2,0},{1,3},{3,1},{4,6},{6,4},{5,7},{7,5},{8,10},{10,8},{9,1... | collective-permute-start | bytes 798728 | tf_op jit(solution)/shard_map/ppermute | solution.py:405

commit v2 on v1

--- a/solution.py
+++ b/solution.py
@@ -31,7 +31,7 @@
 CAP = 8
 NONE = RING * INNER_B
 OVER = 2 * KW
-STEP = 4
+STEP = 8
 LIST = LANES * SLOTS_B + STEP
 
 VMEM = pl.BlockSpec(memory_space=pltpu.VMEM)

time: 51.3 us -> 51.1 us (level)
  transfers between devices with their start and end apart: 9 -> 9, of which waited for: 7 -> 7; matrix products, arithmetic and copies ran while one was open for 0% -> 0% of each run, Pallas kernels for 5% -> 6%
where the time goes in v2:
time: 51.1 us; the launch traced here: 50.5 us
  starting transfers between devices  22.6 us (44%)
  waiting for transfers between devices  17.5 us (34%)
  Pallas kernels  6.66 us (13%)
  between operations  1.91 us (4%)
  local copies, waits for them, and re-layouts  1.72 us (3%)
    all_to_all x1, starting transfers between devices, on_device(): ring = lax.all_to_all(to_ring, ('z', 'pair'), 0, 0)  10.1 us
    all_to_all x1, starting transfers between devices, on_device(): received = lax.all_to_all(to_peers, ('y', 'layer'), 0, 0)  5.86 us
    all_to_all x1, waiting for transfers between devices, on_device(): ring = lax.all_to_all(to_ring, ('z', 'pair'), 0, 0)  5.78 us
    all_to_all x1, waiting for transfers between devices, on_device(): received = lax.all_to_all(to_peers, ('y', 'layer'), 0, 0)  5.35 us
    ppermute x3, starting transfers between devices, on_device(): lax.ppermute(joined, 'y', [(y, (y + k) % SIDE) for y in range(SIDE)])  4.61 us
    ppermute x3, waiting for transfers between devices, on_device(): lax.ppermute(joined, 'y', [(y, (y + k) % SIDE) for y in range(SIDE)])  3.85 us
    pallas_call x1, Pallas kernels, on_device(): pl.pallas_call(select_kernel, out_shape=jax.ShapeDtypeStruct((PEERS, CAP...  2.23 us
    pallas_call x1, Pallas kernels, product_call(): pl.pallas_call(functools.partial(product_kernel, slots, chunks), out_shap...  2.02 us
  transfers between devices with their start and end apart: 9, of which 7 were waited for; matrix products, arithmetic and copies ran while one was open for 0% of the time, Pallas kernels for 6%

profile of v2, /device:TPU:2, one launch (start us, length us, event | category | flops | bytes accessed | tf_op | source)
XLA Modules:
  0.0 50.5 jit_solution(1391223981907499482)
XLA Ops:
  0.7 1.8 %pack.1 = bf16[16,136,128]{2,1,0:T(8,128)(2,1)} custom-call(bf16[4,1,64,64]{3,2,1,0:T(8,128)(2,1)} %b_ref.1, s32[1,2,4]{2,1,0:T(2,128)} %bitcast.4, s32[1,1]{1,0:T(1,128)S(6)} %copy.12.count_ref), custom_call_target="tpu_custom_call" | custom-call | tf_op jit(solution)/shard_map/pack/pallas_call | solution.py:352
  2.5 10.1 %all-to-all-start.1 = ((bf16[16,136,128]{2,1,0:T(8,128)(2,1)}), bf16[16,136,128]{2,1,0:T(8,128)(2,1)S(1)}, u32[]{:S(2)}, u32[]{:S(2)}) async-start(bf16[16,136,128]{2,1,0:T(8,128)(2,1)} %pack.1), calls=%async_computation.1 | async-start | bytes 1114112 | tf_op jit(solution)/shard_map/all_to_all | solution.py:374
  13.3 0.0 copy-start
  13.3 1.0 %copy-done = bf16[1,32,64,64]{3,2,1,0:T(8,128)(2,1)S(1)} copy-done((bf16[1,32,64,64]{3,2,1,0:T(8,128)(2,1)S(1)}, bf16[1,32,64,64]{3,2,1,0:T(8,128)(2,1)}, u32[]{:S(2)}) %copy-start) | copy-done | bytes 262168
  14.3 0.0 copy-start.1
  14.3 0.7 %copy-done.1 = s32[1,32,2]{1,2,0:T(2,128)S(1)} copy-done((s32[1,32,2]{1,2,0:T(2,128)S(1)}, s32[1,32,2]{1,2,0:T(2,128)}, u32[]{:S(2)}) %copy-start.1) | copy-done | bytes 280
  15.0 0.1 pack_a.1
  15.2 1.5 %collective-permute-start.1 = (bf16[1040,128]{1,0:T(8,128)(2,1)S(1)}, bf16[1040,128]{1,0:T(8,128)(2,1)S(1)}, u32[]{:S(2)}, u32[]{:S(2)}) collective-permute-start(bf16[1040,128]{1,0:T(8,128)(2,1)S(1)} %get-tuple-element.32.own_ref), channel_id=1, source_target_pairs={{0,1},{1,0},{2,3},{3,2},{4,5},{5,4},{6,7},{7,6},{8,9},{9,8},{10,11... | collective-permute-start | bytes 798728 | tf_op jit(solution)/shard_map/ppermute | solution.py:386
  16.7 0.0 collective-permute-start.3
  16.7 1.2 %collective-permute-done.3.core_ref = s32[8,128]{1,0:T(8,128)S(1)} collective-permute-done((s32[8,128]{1,0:T(8,128)S(1)}, s32[8,128]{1,0:T(8,128)S(1)}, u32[]{:S(2)}, u32[]{:S(2)}) %collective-permute-start.3) | collective-permute-done | bytes 4128 | tf_op jit(solution)/shard_map/ppermute | solution.py:373
  17.8 3.0 %collective-permute-start.6 = (s32[8,128]{1,0:T(8,128)S(1)}, s32[8,128]{1,0:T(8,128)S(1)}, u32[]{:S(2)}, u32[]{:S(2)}) collective-permute-start(s32[8,128]{1,0:T(8,128)S(1)} %join_keys.1.keys_ref.keys0_ref), channel_id=1, source_target_pairs={{0,24},{8,0},{16,8},{24,16},{1,25},{9,1},{17,9},{25,17},{2,26},{10... | collective-permute-start | bytes 12296 | tf_op jit(solution)/shard_map/ppermute | solution.py:384
  20.9 0.6 %collective-permute-start.5 = (s32[8,128]{1,0:T(8,128)S(1)}, s32[8,128]{1,0:T(8,128)S(1)}, u32[]{:S(2)}, u32[]{:S(2)}) collective-permute-start(s32[8,128]{1,0:T(8,128)S(1)} %join_keys.1.keys_ref.keys0_ref), channel_id=1, source_target_pairs={{0,16},{8,24},{16,0},{24,8},{1,17},{9,25},{17,1},{25,9},{2,18},{10... | collective-permute-start | bytes 12296 | tf_op jit(solution)/shard_map/ppermute | solution.py:384
  21.5 1.0 %collective-permute-start.4 = (s32[8,128]{1,0:T(8,128)S(1)}, s32[8,128]{1,0:T(8,128)S(1)}, u32[]{:S(2)}, u32[]{:S(2)}) collective-permute-start(s32[8,128]{1,0:T(8,128)S(1)} %join_keys.1.keys_ref.keys0_ref), channel_id=1, source_target_pairs={{0,8},{8,16},{16,24},{24,0},{1,9},{9,17},{17,25},{25,1},{2,10},{10... | collective-permute-start | bytes 12296 | tf_op jit(solution)/shard_map/ppermute | solution.py:384
  22.5 0.0 collective-permute-done.6.keys3_ref
  22.5 3.5 %collective-permute-done.5.keys2_ref = s32[8,128]{1,0:T(8,128)S(1)} collective-permute-done((s32[8,128]{1,0:T(8,128)S(1)}, s32[8,128]{1,0:T(8,128)S(1)}, u32[]{:S(2)}, u32[]{:S(2)}) %collective-permute-start.5) | collective-permute-done | bytes 4128 | tf_op jit(solution)/shard_map/ppermute | solution.py:384
  26.0 0.3 collective-permute-done.4.keys1_ref
  26.3 5.8 %all-to-all-done.1.ring_ref = bf16[16,136,128]{2,1,0:T(8,128)(2,1)S(1)} async-done(((bf16[16,136,128]{2,1,0:T(8,128)(2,1)}), bf16[16,136,128]{2,1,0:T(8,128)(2,1)S(1)}, u32[]{:S(2)}, u32[]{:S(2)}) %all-to-all-start.1) | async-done | bytes 557088 | tf_op jit(solution)/shard_map/all_to_all | solution.py:374
  32.1 0.0 copy-start.2
  32.1 2.2 %select.1 = bf16[8,272,128]{2,1,0:T(8,128)(2,1)} custom-call(bf16[16,136,128]{2,1,0:T(8,128)(2,1)S(1)} %all-to-all-done.1.ring_ref, s32[8,128]{1,0:T(8,128)S(1)} %join_keys.1.keys_ref.keys0_ref, s32[8,128]{1,0:T(8,128)S(1)} %collective-permute-done.4.keys1_ref, s32[8,128]{1,0:T(8,128)S(1)} %collective-permute-done.5.keys2_ref, ...), custom_call_target="tpu_custom_call" | custom-call | tf_op jit(solution)/shard_map/select/pallas_call | solution.py:388
  34.3 5.9 %all-to-all-start.2 = ((bf16[8,272,128]{2,1,0:T(8,128)(2,1)}), bf16[8,272,128]{2,1,0:T(8,128)(2,1)S(1)}, u32[]{:S(2)}, u32[]{:S(2)}) async-start(bf16[8,272,128]{2,1,0:T(8,128)(2,1)} %select.1), calls=%async_computation.2 | async-start | bytes 1114112 | tf_op jit(solution)/shard_map/all_to_all | solution.py:403
  40.2 0.0 collective-permute-start
  40.2 0.0 collective-permute-done.1.lay_ref
  40.2 0.5 %collective-permute-start.2 = (bf16[1040,128]{1,0:T(8,128)(2,1)S(1)}, bf16[1040,128]{1,0:T(8,128)(2,1)S(1)}, u32[]{:S(2)}, u32[]{:S(2)}) collective-permute-start(bf16[1040,128]{1,0:T(8,128)(2,1)S(1)} %collective-permute-done.1.lay_ref), channel_id=1, source_target_pairs={{0,2},{2,0},{1,3},{3,1},{4,6},{6,4},{5,7},{7,5},{8,10},{10,8},{9,1... | collective-permute-start | bytes 798728 | tf_op jit(solution)/shard_map/ppermute | solution.py:405
  40.7 1.0 %collective-permute-done.core_ref = bf16[1040,128]{1,0:T(8,128)(2,1)S(1)} collective-permute-done((bf16[1040,128]{1,0:T(8,128)(2,1)S(1)}, bf16[1040,128]{1,0:T(8,128)(2,1)S(1)}, u32[]{:S(2)}, u32[]{:S(2)}) %collective-permute-start) | collective-permute-done | bytes 266272 | tf_op jit(solution)/shard_map/ppermute | solution.py:385
  41.7 0.0 copy-done.2
  41.7 0.4 collective-permute-done.2.diag_ref
  42.1 0.4 unite_a.1
  42.5 5.3 %all-to-all-done.2.b_ref = bf16[8,272,128]{2,1,0:T(8,128)(2,1)S(1)} async-done(((bf16[8,272,128]{2,1,0:T(8,128)(2,1)}), bf16[8,272,128]{2,1,0:T(8,128)(2,1)S(1)}, u32[]{:S(2)}, u32[]{:S(2)}) %all-to-all-start.2) | async-done | bytes 557088 | tf_op jit(solution)/shard_map/all_to_all | solution.py:403
  47.9 2.0 %product_8.1 = (bf16[256,512]{1,0:T(8,128)(2,1)}, s32[1]{0:T(128)}) custom-call(bf16[128,64,128]{2,1,0:T(8,128)(2,1)S(1)} %get-tuple-element.34.a_ref, s32[8,128]{1,0:T(8,128)S(1)} %get-tuple-element.35.keys_ref, bf16[8,272,128]{2,1,0:T(8,128)(2,1)S(1)} %all-to-all-done.2.b_ref), custom_call_target="tpu_custom_call" | custom-call | tf_op jit(solution)/shard_map/product_8/pallas_call | solution.py:325
  (2 shorter events, 0.0 us)
Async XLA Ops:
  2.5 29.6 %all-to-all-start.1 = ((bf16[16,136,128]{2,1,0:T(8,128)(2,1)}), bf16[16,136,128]{2,1,0:T(8,128)(2,1)S(1)}, u32[]{:S(2)}, u32[]{:S(2)}) async-start(bf16[16,136,128]{2,1,0:T(8,128)(2,1)} %pack.1), calls=%async_computation.1 | async-start | bytes 1114112 | tf_op jit(solution)/shard_map/all_to_all | solution.py:374
  13.3 1.0 %copy-start = (bf16[1,32,64,64]{3,2,1,0:T(8,128)(2,1)S(1)}, bf16[1,32,64,64]{3,2,1,0:T(8,128)(2,1)}, u32[]{:S(2)}) copy-start(bf16[1,32,64,64]{3,2,1,0:T(8,128)(2,1)} %a_ref) | copy-start | bytes 786436
  14.3 0.7 %copy-start.1 = (s32[1,32,2]{1,2,0:T(2,128)S(1)}, s32[1,32,2]{1,2,0:T(2,128)}, u32[]{:S(2)}) copy-start(s32[1,32,2]{1,2,0:T(2,128)} %param.9) | copy-start | bytes 772
  15.2 25.0 %collective-permute-start.1 = (bf16[1040,128]{1,0:T(8,128)(2,1)S(1)}, bf16[1040,128]{1,0:T(8,128)(2,1)S(1)}, u32[]{:S(2)}, u32[]{:S(2)}) collective-permute-start(bf16[1040,128]{1,0:T(8,128)(2,1)S(1)} %get-tuple-element.32.own_ref), channel_id=1, source_target_pairs={{0,1},{1,0},{2,3},{3,2},{4,5},{5,4},{6,7},{7,6},{8,9},{9,8},{10,11... | collective-permute-start | bytes 798728 | tf_op jit(solution)/shard_map/ppermute | solution.py:386
  16.7 1.2 %collective-permute-start.3 = (s32[8,128]{1,0:T(8,128)S(1)}, s32[8,128]{1,0:T(8,128)S(1)}, u32[]{:S(2)}, u32[]{:S(2)}) collective-permute-start(s32[8,128]{1,0:T(8,128)S(1)} %get-tuple-element.33.own_ref), channel_id=1, source_target_pairs={{0,2},{2,0},{1,3},{3,1},{4,6},{6,4},{5,7},{7,5},{8,10},{10,8},{9,1... | collective-permute-start | bytes 12296 | tf_op jit(solution)/shard_map/ppermute | solution.py:373
  17.8 4.6 %collective-permute-start.6 = (s32[8,128]{1,0:T(8,128)S(1)}, s32[8,128]{1,0:T(8,128)S(1)}, u32[]{:S(2)}, u32[]{:S(2)}) collective-permute-start(s32[8,128]{1,0:T(8,128)S(1)} %join_keys.1.keys_ref.keys0_ref), channel_id=1, source_target_pairs={{0,24},{8,0},{16,8},{24,16},{1,25},{9,1},{17,9},{25,17},{2,26},{10... | collective-permute-start | bytes 12296 | tf_op jit(solution)/shard_map/ppermute | solution.py:384
  20.9 5.1 %collective-permute-start.5 = (s32[8,128]{1,0:T(8,128)S(1)}, s32[8,128]{1,0:T(8,128)S(1)}, u32[]{:S(2)}, u32[]{:S(2)}) collective-permute-start(s32[8,128]{1,0:T(8,128)S(1)} %join_keys.1.keys_ref.keys0_ref), channel_id=1, source_target_pairs={{0,16},{8,24},{16,0},{24,8},{1,17},{9,25},{17,1},{25,9},{2,18},{10... | collective-permute-start | bytes 12296 | tf_op jit(solution)/shard_map/ppermute | solution.py:384
  21.5 4.8 %collective-permute-start.4 = (s32[8,128]{1,0:T(8,128)S(1)}, s32[8,128]{1,0:T(8,128)S(1)}, u32[]{:S(2)}, u32[]{:S(2)}) collective-permute-start(s32[8,128]{1,0:T(8,128)S(1)} %join_keys.1.keys_ref.keys0_ref), channel_id=1, source_target_pairs={{0,8},{8,16},{16,24},{24,0},{1,9},{9,17},{17,25},{25,1},{2,10},{10... | collective-permute-start | bytes 12296 | tf_op jit(solution)/shard_map/ppermute | solution.py:384
  32.1 9.6 %copy-start.2 = (bf16[16,136,128]{2,1,0:T(8,128)(2,1)}, bf16[16,136,128]{2,1,0:T(8,128)(2,1)S(1)}, u32[]{:S(2)}) copy-start(bf16[16,136,128]{2,1,0:T(8,128)(2,1)S(1)} %all-to-all-done.1.ring_ref) | copy-start | bytes 1671172
  34.3 13.6 %all-to-all-start.2 = ((bf16[8,272,128]{2,1,0:T(8,128)(2,1)}), bf16[8,272,128]{2,1,0:T(8,128)(2,1)S(1)}, u32[]{:S(2)}, u32[]{:S(2)}) async-start(bf16[8,272,128]{2,1,0:T(8,128)(2,1)} %select.1), calls=%async_computation.2 | async-start | bytes 1114112 | tf_op jit(solution)/shard_map/all_to_all | solution.py:403
  40.2 1.5 %collective-permute-start = (bf16[1040,128]{1,0:T(8,128)(2,1)S(1)}, bf16[1040,128]{1,0:T(8,128)(2,1)S(1)}, u32[]{:S(2)}, u32[]{:S(2)}) collective-permute-start(bf16[1040,128]{1,0:T(8,128)(2,1)S(1)} %get-tuple-element.32.own_ref), channel_id=1, source_target_pairs={{0,2},{2,0},{1,3},{3,1},{4,6},{6,4},{5,7},{7,5},{8,10},{10,8},{9,1... | collective-permute-start | bytes 798728 | tf_op jit(solution)/shard_map/ppermute | solution.py:385
  40.2 1.9 %collective-permute-start.2 = (bf16[1040,128]{1,0:T(8,128)(2,1)S(1)}, bf16[1040,128]{1,0:T(8,128)(2,1)S(1)}, u32[]{:S(2)}, u32[]{:S(2)}) collective-permute-start(bf16[1040,128]{1,0:T(8,128)(2,1)S(1)} %collective-permute-done.1.lay_ref), channel_id=1, source_target_pairs={{0,2},{2,0},{1,3},{3,1},{4,6},{6,4},{5,7},{7,5},{8,10},{10,8},{9,1... | collective-permute-start | bytes 798728 | tf_op jit(solution)/shard_map/ppermute | solution.py:405

commit v3 on v2

--- a/solution.py
+++ b/solution.py
@@ -51,7 +51,7 @@
 
 
 def pack_kernel(b_ref, index_ref, count_ref, out_ref, piece):
-    at = lax.axis_index("z") * PAIR + lax.axis_index("pair")
+    at = lax.axis_index("pair") * DEPTH + lax.axis_index("z")
     row = iota((SUB, LANES), 0)
     live = (row & (SLOTS_B - 1)) < jnp.broadcast_to(count_ref[...], (SUB, LANES))
     codes = jnp.where(row < SLOTS_B, float(NONE), 0.0)
@@ -99,13 +99,13 @@
         keys = jnp.where(left, keys, pltpu.roll(keys, BLK, 1))
         mine = (keys >= 0) & (keys >> 12 == half)
         wanted.append(jnp.where(mine, keys & (INNER - 1), -1))
-        low = 1 << (3 * LAYERS * ((y + SIDE - back) & (SIDE - 1)))
-        weight.append(jnp.where(left, low, low << 3))
+        low = 1 << (3 * ((y + SIDE - back) & (SIDE - 1)))
+        weight.append(jnp.where(left, low, low << (3 * SIDE)))
     rows = [jnp.zeros((SUB, LANES), jnp.int32) for _ in range(3)]
     for g in range(RING):
         place = ring_ref[g, PIECE:, :].astype(jnp.float32).astype(jnp.int32)
         column = pltpu.roll(place, SLOTS_B, 0)
-        inner = ((g >> 1 << 3) + y * PAIR + (g & 1)) * INNER_B + (place & (INNER_B - 1))
+        inner = ((g % DEPTH) * SIDE * PAIR + y * PAIR + g // DEPTH) * INNER_B + (place & (INNER_B - 1))
         inner = jnp.where((place < NONE) & (sub < SLOTS_B), inner, -2)
         counts = jnp.zeros((SUB, LANES), jnp.int32)
         for k in range(SIDE):
@@ -229,10 +229,10 @@
         for y in range(SIDE):
             for source in range(LAYERS):
                 at = slots * ROWS + chunk * TAIL
-                tail = b_ref[y * LAYERS + source, at : at + TAIL, :].astype(jnp.float32).astype(jnp.int32)
+                tail = b_ref[source * SIDE + y, at : at + TAIL, :].astype(jnp.float32).astype(jnp.int32)
                 most = jnp.maximum(most, tail[SUB:])
                 place, column = tail[:SUB], tail[SUB:] & (KW - 1)
-                piece = ((place >> 5) << 3) + y * PAIR + ((place >> 4) & 1)
+                piece = (((place >> 4) & (DEPTH - 1)) << 3) + y * PAIR + (place >> 7)
                 found = piece * INNER_B + (place & (INNER_B - 1)) + source * INNER
                 found = jnp.where(place < NONE, found, -2)
                 word = (1 << (3 * SUB + sub)) | (column << (3 * sub))
@@ -260,7 +260,7 @@
     def gather(state):
         i, n = state
         key = info_s[1, i]
-        sender = ((key >> 5) & (SIDE - 1)) * LAYERS + (i >> 6)
+        sender = (i >> 6) * SIDE + ((key >> 5) & (SIDE - 1))
 
         for chunk in range(chunks):
             word = info_s[2 + chunk, i]
@@ -371,7 +371,7 @@
         name="pack_a",
     )(a_blocks, a_index, a_count)
     keys_core = lax.ppermute(keys, "col", swap)
-    ring = lax.all_to_all(to_ring, ("z", "pair"), 0, 0)
+    ring = lax.all_to_all(to_ring, ("pair", "z"), 0, 0)
 
     joined = pl.pallas_call(
         join_kernel,
@@ -400,7 +400,7 @@
         compiler_params=SMALL,
         name="select",
     )(ring, joined, *behind)
-    received = lax.all_to_all(to_peers, ("y", "layer"), 0, 0)
+    received = lax.all_to_all(to_peers, ("layer", "y"), 0, 0)
 
     a_diag = lax.ppermute(a_layer, "col", swap)
     operands = pl.pallas_call(
@@ -433,7 +433,7 @@
             compiler_params=LIMIT,
             name="all_blocks",
         )(ring)
-        everything = lax.all_to_all(to_all, ("y", "layer"), 0, 0)
+        everything = lax.all_to_all(to_all, ("layer", "y"), 0, 0)
         return product_call(SLOTS, SLOTS // SUB, *operands, everything)[0]
 
     return lax.cond(over[0] > 0, whole, chosen, result, ring, *operands)

time: 51.1 us -> 49.1 us (0.961); the launches traced: 50.5 us -> 49 us
  waiting for transfers between devices: 17.5 us -> 15.6 us
    all_to_all x2, waiting for transfers between devices: 11.1 us -> 9.15 us  [the longest x1 5.06 us: on_device(): received = lax.all_to_all(to_peers, ('layer', 'y'), 0, 0)]
where the time goes in v3:
time: 49.1 us; the launch traced here: 49 us
  starting transfers between devices  22.7 us (46%)
  waiting for transfers between devices  15.6 us (32%)
  Pallas kernels  7.11 us (14%)
  between operations  1.91 us (4%)
  local copies, waits for them, and re-layouts  1.72 us (4%)
    all_to_all x1, starting transfers between devices, on_device(): ring = lax.all_to_all(to_ring, ('pair', 'z'), 0, 0)  10.1 us
    all_to_all x1, starting transfers between devices, on_device(): received = lax.all_to_all(to_peers, ('layer', 'y'), 0, 0)  5.9 us
    all_to_all x1, waiting for transfers between devices, on_device(): received = lax.all_to_all(to_peers, ('layer', 'y'), 0, 0)  5.06 us
    ppermute x3, starting transfers between devices, on_device(): lax.ppermute(joined, 'y', [(y, (y + k) % SIDE) for y in range(SIDE)])  4.61 us
    all_to_all x1, waiting for transfers between devices, on_device(): ring = lax.all_to_all(to_ring, ('pair', 'z'), 0, 0)  4.1 us
    ppermute x3, waiting for transfers between devices, on_device(): lax.ppermute(joined, 'y', [(y, (y + k) % SIDE) for y in range(SIDE)])  3.85 us
    pallas_call x1, Pallas kernels, product_call(): pl.pallas_call(functools.partial(product_kernel, slots, chunks), out_shap...  2.42 us
    pallas_call x1, Pallas kernels, on_device(): pl.pallas_call(select_kernel, out_shape=jax.ShapeDtypeStruct((PEERS, CAP...  2.28 us
  transfers between devices with their start and end apart: 9, of which 7 were waited for; matrix products, arithmetic and copies ran while one was open for 0% of the time, Pallas kernels for 6%

profile of v3, /device:TPU:2, one launch (start us, length us, event | category | flops | bytes accessed | tf_op | source)
XLA Modules:
  0.0 49.0 jit_solution(17387969642911906843)
XLA Ops:
  0.7 1.8 %pack.1 = bf16[16,136,128]{2,1,0:T(8,128)(2,1)} custom-call(bf16[4,1,64,64]{3,2,1,0:T(8,128)(2,1)} %b_ref.1, s32[1,2,4]{2,1,0:T(2,128)} %bitcast.4, s32[1,1]{1,0:T(1,128)S(6)} %copy.12.count_ref), custom_call_target="tpu_custom_call" | custom-call | tf_op jit(solution)/shard_map/pack/pallas_call | solution.py:352
  2.5 10.1 %all-to-all-start.1 = ((bf16[16,136,128]{2,1,0:T(8,128)(2,1)}), bf16[16,136,128]{2,1,0:T(8,128)(2,1)S(1)}, u32[]{:S(2)}, u32[]{:S(2)}) async-start(bf16[16,136,128]{2,1,0:T(8,128)(2,1)} %pack.1), calls=%async_computation.1 | async-start | bytes 1114112 | tf_op jit(solution)/shard_map/all_to_all | solution.py:374
  13.3 0.0 copy-start
  13.3 1.0 %copy-done = bf16[1,32,64,64]{3,2,1,0:T(8,128)(2,1)S(1)} copy-done((bf16[1,32,64,64]{3,2,1,0:T(8,128)(2,1)S(1)}, bf16[1,32,64,64]{3,2,1,0:T(8,128)(2,1)}, u32[]{:S(2)}) %copy-start) | copy-done | bytes 262168
  14.3 0.0 copy-start.1
  14.3 0.7 %copy-done.1 = s32[1,32,2]{1,2,0:T(2,128)S(1)} copy-done((s32[1,32,2]{1,2,0:T(2,128)S(1)}, s32[1,32,2]{1,2,0:T(2,128)}, u32[]{:S(2)}) %copy-start.1) | copy-done | bytes 280
  15.0 0.1 pack_a.1
  15.2 1.5 %collective-permute-start.1 = (bf16[1040,128]{1,0:T(8,128)(2,1)S(1)}, bf16[1040,128]{1,0:T(8,128)(2,1)S(1)}, u32[]{:S(2)}, u32[]{:S(2)}) collective-permute-start(bf16[1040,128]{1,0:T(8,128)(2,1)S(1)} %get-tuple-element.32.own_ref), channel_id=1, source_target_pairs={{0,1},{1,0},{2,3},{3,2},{4,5},{5,4},{6,7},{7,6},{8,9},{9,8},{10,11... | collective-permute-start | bytes 798728 | tf_op jit(solution)/shard_map/ppermute | solution.py:386
  16.7 0.0 collective-permute-start.3
  16.7 1.2 %collective-permute-done.3.core_ref = s32[8,128]{1,0:T(8,128)S(1)} collective-permute-done((s32[8,128]{1,0:T(8,128)S(1)}, s32[8,128]{1,0:T(8,128)S(1)}, u32[]{:S(2)}, u32[]{:S(2)}) %collective-permute-start.3) | collective-permute-done | bytes 4128 | tf_op jit(solution)/shard_map/ppermute | solution.py:373
  17.8 3.0 %collective-permute-start.6 = (s32[8,128]{1,0:T(8,128)S(1)}, s32[8,128]{1,0:T(8,128)S(1)}, u32[]{:S(2)}, u32[]{:S(2)}) collective-permute-start(s32[8,128]{1,0:T(8,128)S(1)} %join_keys.1.keys_ref.keys0_ref), channel_id=1, source_target_pairs={{0,24},{8,0},{16,8},{24,16},{1,25},{9,1},{17,9},{25,17},{2,26},{10... | collective-permute-start | bytes 12296 | tf_op jit(solution)/shard_map/ppermute | solution.py:384
  20.9 0.6 %collective-permute-start.5 = (s32[8,128]{1,0:T(8,128)S(1)}, s32[8,128]{1,0:T(8,128)S(1)}, u32[]{:S(2)}, u32[]{:S(2)}) collective-permute-start(s32[8,128]{1,0:T(8,128)S(1)} %join_keys.1.keys_ref.keys0_ref), channel_id=1, source_target_pairs={{0,16},{8,24},{16,0},{24,8},{1,17},{9,25},{17,1},{25,9},{2,18},{10... | collective-permute-start | bytes 12296 | tf_op jit(solution)/shard_map/ppermute | solution.py:384
  21.5 1.0 %collective-permute-start.4 = (s32[8,128]{1,0:T(8,128)S(1)}, s32[8,128]{1,0:T(8,128)S(1)}, u32[]{:S(2)}, u32[]{:S(2)}) collective-permute-start(s32[8,128]{1,0:T(8,128)S(1)} %join_keys.1.keys_ref.keys0_ref), channel_id=1, source_target_pairs={{0,8},{8,16},{16,24},{24,0},{1,9},{9,17},{17,25},{25,1},{2,10},{10... | collective-permute-start | bytes 12296 | tf_op jit(solution)/shard_map/ppermute | solution.py:384
  22.5 0.0 collective-permute-done.6.keys3_ref
  22.5 3.5 %collective-permute-done.5.keys2_ref = s32[8,128]{1,0:T(8,128)S(1)} collective-permute-done((s32[8,128]{1,0:T(8,128)S(1)}, s32[8,128]{1,0:T(8,128)S(1)}, u32[]{:S(2)}, u32[]{:S(2)}) %collective-permute-start.5) | collective-permute-done | bytes 4128 | tf_op jit(solution)/shard_map/ppermute | solution.py:384
  26.0 0.3 collective-permute-done.4.keys1_ref
  26.3 4.1 %all-to-all-done.1.ring_ref = bf16[16,136,128]{2,1,0:T(8,128)(2,1)S(1)} async-done(((bf16[16,136,128]{2,1,0:T(8,128)(2,1)}), bf16[16,136,128]{2,1,0:T(8,128)(2,1)S(1)}, u32[]{:S(2)}, u32[]{:S(2)}) %all-to-all-start.1) | async-done | bytes 557088 | tf_op jit(solution)/shard_map/all_to_all | solution.py:374
  30.4 0.0 copy-start.2
  30.4 2.3 %select.1 = bf16[8,272,128]{2,1,0:T(8,128)(2,1)} custom-call(bf16[16,136,128]{2,1,0:T(8,128)(2,1)S(1)} %all-to-all-done.1.ring_ref, s32[8,128]{1,0:T(8,128)S(1)} %join_keys.1.keys_ref.keys0_ref, s32[8,128]{1,0:T(8,128)S(1)} %collective-permute-done.4.keys1_ref, s32[8,128]{1,0:T(8,128)S(1)} %collective-permute-done.5.keys2_ref, ...), custom_call_target="tpu_custom_call" | custom-call | tf_op jit(solution)/shard_map/select/pallas_call | solution.py:388
  32.7 5.9 %all-to-all-start.2 = ((bf16[8,272,128]{2,1,0:T(8,128)(2,1)}), bf16[8,272,128]{2,1,0:T(8,128)(2,1)S(1)}, u32[]{:S(2)}, u32[]{:S(2)}) async-start(bf16[8,272,128]{2,1,0:T(8,128)(2,1)} %select.1), calls=%async_computation.2 | async-start | bytes 1114112 | tf_op jit(solution)/shard_map/all_to_all | solution.py:403
  38.6 0.0 collective-permute-start
  38.6 0.0 collective-permute-done.1.lay_ref
  38.6 0.5 %collective-permute-start.2 = (bf16[1040,128]{1,0:T(8,128)(2,1)S(1)}, bf16[1040,128]{1,0:T(8,128)(2,1)S(1)}, u32[]{:S(2)}, u32[]{:S(2)}) collective-permute-start(bf16[1040,128]{1,0:T(8,128)(2,1)S(1)} %collective-permute-done.1.lay_ref), channel_id=1, source_target_pairs={{0,2},{2,0},{1,3},{3,1},{4,6},{6,4},{5,7},{7,5},{8,10},{10,8},{9,1... | collective-permute-start | bytes 798728 | tf_op jit(solution)/shard_map/ppermute | solution.py:405
  39.1 1.0 %collective-permute-done.core_ref = bf16[1040,128]{1,0:T(8,128)(2,1)S(1)} collective-permute-done((bf16[1040,128]{1,0:T(8,128)(2,1)S(1)}, bf16[1040,128]{1,0:T(8,128)(2,1)S(1)}, u32[]{:S(2)}, u32[]{:S(2)}) %collective-permute-start) | collective-permute-done | bytes 266272 | tf_op jit(solution)/shard_map/ppermute | solution.py:385
  40.1 0.0 copy-done.2
  40.1 0.4 collective-permute-done.2.diag_ref
  40.5 0.4 unite_a.1
  40.9 5.1 %all-to-all-done.2.b_ref = bf16[8,272,128]{2,1,0:T(8,128)(2,1)S(1)} async-done(((bf16[8,272,128]{2,1,0:T(8,128)(2,1)}), bf16[8,272,128]{2,1,0:T(8,128)(2,1)S(1)}, u32[]{:S(2)}, u32[]{:S(2)}) %all-to-all-start.2) | async-done | bytes 557088 | tf_op jit(solution)/shard_map/all_to_all | solution.py:403
  46.0 2.4 %product_8.1 = (bf16[256,512]{1,0:T(8,128)(2,1)}, s32[1]{0:T(128)}) custom-call(bf16[128,64,128]{2,1,0:T(8,128)(2,1)S(1)} %get-tuple-element.34.a_ref, s32[8,128]{1,0:T(8,128)S(1)} %get-tuple-element.35.keys_ref, bf16[8,272,128]{2,1,0:T(8,128)(2,1)S(1)} %all-to-all-done.2.b_ref), custom_call_target="tpu_custom_call" | custom-call | tf_op jit(solution)/shard_map/product_8/pallas_call | solution.py:325
  (2 shorter events, 0.0 us)
Async XLA Ops:
  2.5 27.9 %all-to-all-start.1 = ((bf16[16,136,128]{2,1,0:T(8,128)(2,1)}), bf16[16,136,128]{2,1,0:T(8,128)(2,1)S(1)}, u32[]{:S(2)}, u32[]{:S(2)}) async-start(bf16[16,136,128]{2,1,0:T(8,128)(2,1)} %pack.1), calls=%async_computation.1 | async-start | bytes 1114112 | tf_op jit(solution)/shard_map/all_to_all | solution.py:374
  13.3 1.0 %copy-start = (bf16[1,32,64,64]{3,2,1,0:T(8,128)(2,1)S(1)}, bf16[1,32,64,64]{3,2,1,0:T(8,128)(2,1)}, u32[]{:S(2)}) copy-start(bf16[1,32,64,64]{3,2,1,0:T(8,128)(2,1)} %a_ref) | copy-start | bytes 786436
  14.3 0.7 %copy-start.1 = (s32[1,32,2]{1,2,0:T(2,128)S(1)}, s32[1,32,2]{1,2,0:T(2,128)}, u32[]{:S(2)}) copy-start(s32[1,32,2]{1,2,0:T(2,128)} %param.9) | copy-start | bytes 772
  15.2 23.4 %collective-permute-start.1 = (bf16[1040,128]{1,0:T(8,128)(2,1)S(1)}, bf16[1040,128]{1,0:T(8,128)(2,1)S(1)}, u32[]{:S(2)}, u32[]{:S(2)}) collective-permute-start(bf16[1040,128]{1,0:T(8,128)(2,1)S(1)} %get-tuple-element.32.own_ref), channel_id=1, source_target_pairs={{0,1},{1,0},{2,3},{3,2},{4,5},{5,4},{6,7},{7,6},{8,9},{9,8},{10,11... | collective-permute-start | bytes 798728 | tf_op jit(solution)/shard_map/ppermute | solution.py:386
  16.7 1.2 %collective-permute-start.3 = (s32[8,128]{1,0:T(8,128)S(1)}, s32[8,128]{1,0:T(8,128)S(1)}, u32[]{:S(2)}, u32[]{:S(2)}) collective-permute-start(s32[8,128]{1,0:T(8,128)S(1)} %get-tuple-element.33.own_ref), channel_id=1, source_target_pairs={{0,2},{2,0},{1,3},{3,1},{4,6},{6,4},{5,7},{7,5},{8,10},{10,8},{9,1... | collective-permute-start | bytes 12296 | tf_op jit(solution)/shard_map/ppermute | solution.py:373
  17.8 4.6 %collective-permute-start.6 = (s32[8,128]{1,0:T(8,128)S(1)}, s32[8,128]{1,0:T(8,128)S(1)}, u32[]{:S(2)}, u32[]{:S(2)}) collective-permute-start(s32[8,128]{1,0:T(8,128)S(1)} %join_keys.1.keys_ref.keys0_ref), channel_id=1, source_target_pairs={{0,24},{8,0},{16,8},{24,16},{1,25},{9,1},{17,9},{25,17},{2,26},{10... | collective-permute-start | bytes 12296 | tf_op jit(solution)/shard_map/ppermute | solution.py:384
  20.9 5.1 %collective-permute-start.5 = (s32[8,128]{1,0:T(8,128)S(1)}, s32[8,128]{1,0:T(8,128)S(1)}, u32[]{:S(2)}, u32[]{:S(2)}) collective-permute-start(s32[8,128]{1,0:T(8,128)S(1)} %join_keys.1.keys_ref.keys0_ref), channel_id=1, source_target_pairs={{0,16},{8,24},{16,0},{24,8},{1,17},{9,25},{17,1},{25,9},{2,18},{10... | collective-permute-start | bytes 12296 | tf_op jit(solution)/shard_map/ppermute | solution.py:384
  21.5 4.8 %collective-permute-start.4 = (s32[8,128]{1,0:T(8,128)S(1)}, s32[8,128]{1,0:T(8,128)S(1)}, u32[]{:S(2)}, u32[]{:S(2)}) collective-permute-start(s32[8,128]{1,0:T(8,128)S(1)} %join_keys.1.keys_ref.keys0_ref), channel_id=1, source_target_pairs={{0,8},{8,16},{16,24},{24,0},{1,9},{9,17},{17,25},{25,1},{2,10},{10... | collective-permute-start | bytes 12296 | tf_op jit(solution)/shard_map/ppermute | solution.py:384
  30.4 9.7 %copy-start.2 = (bf16[16,136,128]{2,1,0:T(8,128)(2,1)}, bf16[16,136,128]{2,1,0:T(8,128)(2,1)S(1)}, u32[]{:S(2)}) copy-start(bf16[16,136,128]{2,1,0:T(8,128)(2,1)S(1)} %all-to-all-done.1.ring_ref) | copy-start | bytes 1671172
  32.7 13.3 %all-to-all-start.2 = ((bf16[8,272,128]{2,1,0:T(8,128)(2,1)}), bf16[8,272,128]{2,1,0:T(8,128)(2,1)S(1)}, u32[]{:S(2)}, u32[]{:S(2)}) async-start(bf16[8,272,128]{2,1,0:T(8,128)(2,1)} %select.1), calls=%async_computation.2 | async-start | bytes 1114112 | tf_op jit(solution)/shard_map/all_to_all | solution.py:403
  38.6 1.5 %collective-permute-start = (bf16[1040,128]{1,0:T(8,128)(2,1)S(1)}, bf16[1040,128]{1,0:T(8,128)(2,1)S(1)}, u32[]{:S(2)}, u32[]{:S(2)}) collective-permute-start(bf16[1040,128]{1,0:T(8,128)(2,1)S(1)} %get-tuple-element.32.own_ref), channel_id=1, source_target_pairs={{0,2},{2,0},{1,3},{3,1},{4,6},{6,4},{5,7},{7,5},{8,10},{10,8},{9,1... | collective-permute-start | bytes 798728 | tf_op jit(solution)/shard_map/ppermute | solution.py:385
  38.6 1.9 %collective-permute-start.2 = (bf16[1040,128]{1,0:T(8,128)(2,1)S(1)}, bf16[1040,128]{1,0:T(8,128)(2,1)S(1)}, u32[]{:S(2)}, u32[]{:S(2)}) collective-permute-start(bf16[1040,128]{1,0:T(8,128)(2,1)S(1)} %collective-permute-done.1.lay_ref), channel_id=1, source_target_pairs={{0,2},{2,0},{1,3},{3,1},{4,6},{6,4},{5,7},{7,5},{8,10},{10,8},{9,1... | collective-permute-start | bytes 798728 | tf_op jit(solution)/shard_map/ppermute | solution.py:405

commit v4 on v3

--- a/solution.py
+++ b/solution.py
@@ -118,7 +118,7 @@
         info_v[k : k + 1, :] = jnp.sum(rows[k], axis=0, keepdims=True)
     copy = pltpu.make_async_copy(info_v, info_s, sem)
     copy.start()
-    none = jnp.where(iota((TAIL, LANES), 0) < SUB, float(NONE), 0.0)
+    none = jnp.where(left, float(NONE), 0.0)
     for d in range(PEERS):
         codes[d] = none
     for d in range(PEERS + 1):
@@ -147,8 +147,7 @@
                             @pl.when(p < CAP)
                             def _():
                                 out_ref[d, pl.ds(pl.multiple_of(p * ROWS, ROWS), ROWS), :] = block
-                                codes[d, pl.ds(p, 1), :] = place
-                                codes[d, pl.ds(SUB + p, 1), :] = column
+                                codes[d, pl.ds(p, 1), :] = jnp.where(left[0:1], place, column)
 
                             @pl.when(p >= CAP)
                             def _():
@@ -157,7 +156,7 @@
         return carry
 
     lax.fori_loop(0, RING, some, 0)
-    over = jnp.where(iota((TAIL, LANES), 0) < SUB, 0, cnt[PEERS] * OVER).astype(jnp.float32)
+    over = jnp.where(left, 0, cnt[PEERS] * OVER).astype(jnp.float32)
     for d in range(PEERS):
         out_ref[d, CAP * ROWS :, :] = (codes[d] + over).astype(jnp.bfloat16)
 
@@ -170,8 +169,9 @@
         tails = [ring_ref[2 * chunk + k, PIECE:, :].astype(jnp.float32) for k in range(2)]
         places = jnp.where(first, tails[0], pltpu.roll(tails[1], SLOTS_B, 0))
         columns = jnp.where(first, pltpu.roll(tails[0], SLOTS_B, 0), tails[1])
+        both = jnp.where(iota((SUB, LANES), 1) < BLK, places, columns)
         at = RING * PIECE + chunk * TAIL
-        message[at : at + TAIL, :] = jnp.concatenate([places, columns], axis=0).astype(jnp.bfloat16)
+        message[at : at + TAIL, :] = jnp.concatenate([both, both], axis=0).astype(jnp.bfloat16)
     copies = [pltpu.make_async_copy(message, out_ref.at[d], sems.at[d]) for d in range(PEERS)]
     for copy in copies:
         copy.start()
@@ -229,9 +229,12 @@
         for y in range(SIDE):
             for source in range(LAYERS):
                 at = slots * ROWS + chunk * TAIL
-                tail = b_ref[source * SIDE + y, at : at + TAIL, :].astype(jnp.float32).astype(jnp.int32)
-                most = jnp.maximum(most, tail[SUB:])
-                place, column = tail[:SUB], tail[SUB:] & (KW - 1)
+                tail = b_ref[source * SIDE + y, at : at + SUB, :].astype(jnp.float32).astype(jnp.int32)
+                turned = pltpu.roll(tail, BLK, 1)
+                place = jnp.where(lane < BLK, tail, turned)
+                column = jnp.where(lane < BLK, turned, tail)
+                most = jnp.maximum(most, column)
+                column = column & (KW - 1)
                 piece = (((place >> 4) & (DEPTH - 1)) << 3) + y * PAIR + (place >> 7)
                 found = piece * INNER_B + (place & (INNER_B - 1)) + source * INNER
                 found = jnp.where(place < NONE, found, -2)
@@ -387,11 +390,11 @@
 
     to_peers = pl.pallas_call(
         select_kernel,
-        out_shape=jax.ShapeDtypeStruct((PEERS, CAP * ROWS + TAIL, LANES), jnp.bfloat16),
+        out_shape=jax.ShapeDtypeStruct((PEERS, CAP * ROWS + SUB, LANES), jnp.bfloat16),
         in_specs=[VMEM] * 5,
         out_specs=VMEM,
         scratch_shapes=[
-            pltpu.VMEM((PEERS, TAIL, LANES), jnp.float32),
+            pltpu.VMEM((PEERS, SUB, LANES), jnp.float32),
             pltpu.VMEM((SUB, LANES), jnp.int32),
             pltpu.SMEM((SUB, LANES), jnp.int32),
             pltpu.SMEM((PEERS + 1,), jnp.int32),

time: 49.1 us -> 49 us (level)
  Pallas kernels: 7.11 us -> 6.43 us
  transfers between devices with their start and end apart: 9 -> 9, of which waited for: 7 -> 7; matrix products, arithmetic and copies ran while one was open for 0% -> 0% of each run, Pallas kernels for 6% -> 5%
where the time goes in v4:
time: 49 us; the launch traced here: 48.5 us
  starting transfers between devices  23 us (47%)
  waiting for transfers between devices  15.5 us (32%)
  Pallas kernels  6.43 us (13%)
  between operations  1.91 us (4%)
  local copies, waits for them, and re-layouts  1.72 us (4%)
    all_to_all x1, starting transfers between devices, on_device(): ring = lax.all_to_all(to_ring, ('pair', 'z'), 0, 0)  10.1 us
    all_to_all x1, starting transfers between devices, on_device(): received = lax.all_to_all(to_peers, ('layer', 'y'), 0, 0)  6.21 us
    all_to_all x1, waiting for transfers between devices, on_device(): received = lax.all_to_all(to_peers, ('layer', 'y'), 0, 0)  4.97 us
    ppermute x3, starting transfers between devices, on_device(): lax.ppermute(joined, 'y', [(y, (y + k) % SIDE) for y in range(SIDE)])  4.61 us
    all_to_all x1, waiting for transfers between devices, on_device(): ring = lax.all_to_all(to_ring, ('pair', 'z'), 0, 0)  4.1 us
    ppermute x3, waiting for transfers between devices, on_device(): lax.ppermute(joined, 'y', [(y, (y + k) % SIDE) for y in range(SIDE)])  3.85 us
    pallas_call x1, Pallas kernels, product_call(): pl.pallas_call(functools.partial(product_kernel, slots, chunks), out_shap...  2.01 us
    pallas_call x1, Pallas kernels, on_device(): pl.pallas_call(select_kernel, out_shape=jax.ShapeDtypeStruct((PEERS, CAP...  2 us
  transfers between devices with their start and end apart: 9, of which 7 were waited for; matrix products, arithmetic and copies ran while one was open for 0% of the time, Pallas kernels for 5%

profile of v4, /device:TPU:2, one launch (start us, length us, event | category | flops | bytes accessed | tf_op | source)
XLA Modules:
  0.0 48.5 jit_solution(11026636752245527645)
XLA Ops:
  0.7 1.8 %pack.1 = bf16[16,136,128]{2,1,0:T(8,128)(2,1)} custom-call(bf16[4,1,64,64]{3,2,1,0:T(8,128)(2,1)} %b_ref.1, s32[1,2,4]{2,1,0:T(2,128)} %bitcast.4, s32[1,1]{1,0:T(1,128)S(6)} %copy.12.count_ref), custom_call_target="tpu_custom_call" | custom-call | tf_op jit(solution)/shard_map/pack/pallas_call | solution.py:355
  2.5 10.1 %all-to-all-start.1 = ((bf16[16,136,128]{2,1,0:T(8,128)(2,1)}), bf16[16,136,128]{2,1,0:T(8,128)(2,1)S(1)}, u32[]{:S(2)}, u32[]{:S(2)}) async-start(bf16[16,136,128]{2,1,0:T(8,128)(2,1)} %pack.1), calls=%async_computation.1 | async-start | bytes 1114112 | tf_op jit(solution)/shard_map/all_to_all | solution.py:377
  13.3 0.0 copy-start
  13.3 1.0 %copy-done = bf16[1,32,64,64]{3,2,1,0:T(8,128)(2,1)S(1)} copy-done((bf16[1,32,64,64]{3,2,1,0:T(8,128)(2,1)S(1)}, bf16[1,32,64,64]{3,2,1,0:T(8,128)(2,1)}, u32[]{:S(2)}) %copy-start) | copy-done | bytes 262168
  14.3 0.0 copy-start.1
  14.3 0.7 %copy-done.1 = s32[1,32,2]{1,2,0:T(2,128)S(1)} copy-done((s32[1,32,2]{1,2,0:T(2,128)S(1)}, s32[1,32,2]{1,2,0:T(2,128)}, u32[]{:S(2)}) %copy-start.1) | copy-done | bytes 280
  15.0 0.1 pack_a.1
  15.2 1.5 %collective-permute-start.1 = (bf16[1040,128]{1,0:T(8,128)(2,1)S(1)}, bf16[1040,128]{1,0:T(8,128)(2,1)S(1)}, u32[]{:S(2)}, u32[]{:S(2)}) collective-permute-start(bf16[1040,128]{1,0:T(8,128)(2,1)S(1)} %get-tuple-element.32.own_ref), channel_id=1, source_target_pairs={{0,1},{1,0},{2,3},{3,2},{4,5},{5,4},{6,7},{7,6},{8,9},{9,8},{10,11... | collective-permute-start | bytes 798728 | tf_op jit(solution)/shard_map/ppermute | solution.py:389
  16.7 0.0 collective-permute-start.3
  16.7 1.2 %collective-permute-done.3.core_ref = s32[8,128]{1,0:T(8,128)S(1)} collective-permute-done((s32[8,128]{1,0:T(8,128)S(1)}, s32[8,128]{1,0:T(8,128)S(1)}, u32[]{:S(2)}, u32[]{:S(2)}) %collective-permute-start.3) | collective-permute-done | bytes 4128 | tf_op jit(solution)/shard_map/ppermute | solution.py:376
  17.8 3.0 %collective-permute-start.6 = (s32[8,128]{1,0:T(8,128)S(1)}, s32[8,128]{1,0:T(8,128)S(1)}, u32[]{:S(2)}, u32[]{:S(2)}) collective-permute-start(s32[8,128]{1,0:T(8,128)S(1)} %join_keys.1.keys_ref.keys0_ref), channel_id=1, source_target_pairs={{0,24},{8,0},{16,8},{24,16},{1,25},{9,1},{17,9},{25,17},{2,26},{10... | collective-permute-start | bytes 12296 | tf_op jit(solution)/shard_map/ppermute | solution.py:387
  20.9 0.6 %collective-permute-start.5 = (s32[8,128]{1,0:T(8,128)S(1)}, s32[8,128]{1,0:T(8,128)S(1)}, u32[]{:S(2)}, u32[]{:S(2)}) collective-permute-start(s32[8,128]{1,0:T(8,128)S(1)} %join_keys.1.keys_ref.keys0_ref), channel_id=1, source_target_pairs={{0,16},{8,24},{16,0},{24,8},{1,17},{9,25},{17,1},{25,9},{2,18},{10... | collective-permute-start | bytes 12296 | tf_op jit(solution)/shard_map/ppermute | solution.py:387
  21.5 1.0 %collective-permute-start.4 = (s32[8,128]{1,0:T(8,128)S(1)}, s32[8,128]{1,0:T(8,128)S(1)}, u32[]{:S(2)}, u32[]{:S(2)}) collective-permute-start(s32[8,128]{1,0:T(8,128)S(1)} %join_keys.1.keys_ref.keys0_ref), channel_id=1, source_target_pairs={{0,8},{8,16},{16,24},{24,0},{1,9},{9,17},{17,25},{25,1},{2,10},{10... | collective-permute-start | bytes 12296 | tf_op jit(solution)/shard_map/ppermute | solution.py:387
  22.5 0.0 collective-permute-done.6.keys3_ref
  22.5 3.5 %collective-permute-done.5.keys2_ref = s32[8,128]{1,0:T(8,128)S(1)} collective-permute-done((s32[8,128]{1,0:T(8,128)S(1)}, s32[8,128]{1,0:T(8,128)S(1)}, u32[]{:S(2)}, u32[]{:S(2)}) %collective-permute-start.5) | collective-permute-done | bytes 4128 | tf_op jit(solution)/shard_map/ppermute | solution.py:387
  26.0 0.3 collective-permute-done.4.keys1_ref
  26.3 4.1 %all-to-all-done.1.ring_ref = bf16[16,136,128]{2,1,0:T(8,128)(2,1)S(1)} async-done(((bf16[16,136,128]{2,1,0:T(8,128)(2,1)}), bf16[16,136,128]{2,1,0:T(8,128)(2,1)S(1)}, u32[]{:S(2)}, u32[]{:S(2)}) %all-to-all-start.1) | async-done | bytes 557088 | tf_op jit(solution)/shard_map/all_to_all | solution.py:377
  30.4 0.0 copy-start.2
  30.4 2.0 %select.1 = bf16[8,264,128]{2,1,0:T(8,128)(2,1)} custom-call(bf16[16,136,128]{2,1,0:T(8,128)(2,1)S(1)} %all-to-all-done.1.ring_ref, s32[8,128]{1,0:T(8,128)S(1)} %join_keys.1.keys_ref.keys0_ref, s32[8,128]{1,0:T(8,128)S(1)} %collective-permute-done.4.keys1_ref, s32[8,128]{1,0:T(8,128)S(1)} %collective-permute-done.5.keys2_ref, ...), custom_call_target="tpu_custom_call" | custom-call | tf_op jit(solution)/shard_map/select/pallas_call | solution.py:391
  32.4 6.2 %all-to-all-start.2 = ((bf16[8,264,128]{2,1,0:T(8,128)(2,1)}), bf16[8,264,128]{2,1,0:T(8,128)(2,1)S(1)}, u32[]{:S(2)}, u32[]{:S(2)}) async-start(bf16[8,264,128]{2,1,0:T(8,128)(2,1)} %select.1), calls=%async_computation.2 | async-start | bytes 1081344 | tf_op jit(solution)/shard_map/all_to_all | solution.py:406
  38.6 0.0 collective-permute-start
  38.6 0.0 collective-permute-done.1.lay_ref
  38.6 0.5 %collective-permute-start.2 = (bf16[1040,128]{1,0:T(8,128)(2,1)S(1)}, bf16[1040,128]{1,0:T(8,128)(2,1)S(1)}, u32[]{:S(2)}, u32[]{:S(2)}) collective-permute-start(bf16[1040,128]{1,0:T(8,128)(2,1)S(1)} %collective-permute-done.1.lay_ref), channel_id=1, source_target_pairs={{0,2},{2,0},{1,3},{3,1},{4,6},{6,4},{5,7},{7,5},{8,10},{10,8},{9,1... | collective-permute-start | bytes 798728 | tf_op jit(solution)/shard_map/ppermute | solution.py:408
  39.1 1.0 %collective-permute-done.core_ref = bf16[1040,128]{1,0:T(8,128)(2,1)S(1)} collective-permute-done((bf16[1040,128]{1,0:T(8,128)(2,1)S(1)}, bf16[1040,128]{1,0:T(8,128)(2,1)S(1)}, u32[]{:S(2)}, u32[]{:S(2)}) %collective-permute-start) | collective-permute-done | bytes 266272 | tf_op jit(solution)/shard_map/ppermute | solution.py:388
  40.2 0.0 copy-done.2
  40.2 0.4 collective-permute-done.2.diag_ref
  40.5 0.4 unite_a.1
  41.0 5.0 %all-to-all-done.2.b_ref = bf16[8,264,128]{2,1,0:T(8,128)(2,1)S(1)} async-done(((bf16[8,264,128]{2,1,0:T(8,128)(2,1)}), bf16[8,264,128]{2,1,0:T(8,128)(2,1)S(1)}, u32[]{:S(2)}, u32[]{:S(2)}) %all-to-all-start.2) | async-done | bytes 540704 | tf_op jit(solution)/shard_map/all_to_all | solution.py:406
  45.9 2.0 %product_8.1 = (bf16[256,512]{1,0:T(8,128)(2,1)}, s32[1]{0:T(128)}) custom-call(bf16[128,64,128]{2,1,0:T(8,128)(2,1)S(1)} %get-tuple-element.34.a_ref, s32[8,128]{1,0:T(8,128)S(1)} %get-tuple-element.35.keys_ref, bf16[8,264,128]{2,1,0:T(8,128)(2,1)S(1)} %all-to-all-done.2.b_ref), custom_call_target="tpu_custom_call" | custom-call | tf_op jit(solution)/shard_map/product_8/pallas_call | solution.py:328
  (2 shorter events, 0.0 us)
Async XLA Ops:
  2.5 27.9 %all-to-all-start.1 = ((bf16[16,136,128]{2,1,0:T(8,128)(2,1)}), bf16[16,136,128]{2,1,0:T(8,128)(2,1)S(1)}, u32[]{:S(2)}, u32[]{:S(2)}) async-start(bf16[16,136,128]{2,1,0:T(8,128)(2,1)} %pack.1), calls=%async_computation.1 | async-start | bytes 1114112 | tf_op jit(solution)/shard_map/all_to_all | solution.py:377
  13.3 1.0 %copy-start = (bf16[1,32,64,64]{3,2,1,0:T(8,128)(2,1)S(1)}, bf16[1,32,64,64]{3,2,1,0:T(8,128)(2,1)}, u32[]{:S(2)}) copy-start(bf16[1,32,64,64]{3,2,1,0:T(8,128)(2,1)} %a_ref) | copy-start | bytes 786436
  14.3 0.7 %copy-start.1 = (s32[1,32,2]{1,2,0:T(2,128)S(1)}, s32[1,32,2]{1,2,0:T(2,128)}, u32[]{:S(2)}) copy-start(s32[1,32,2]{1,2,0:T(2,128)} %param.9) | copy-start | bytes 772
  15.2 23.5 %collective-permute-start.1 = (bf16[1040,128]{1,0:T(8,128)(2,1)S(1)}, bf16[1040,128]{1,0:T(8,128)(2,1)S(1)}, u32[]{:S(2)}, u32[]{:S(2)}) collective-permute-start(bf16[1040,128]{1,0:T(8,128)(2,1)S(1)} %get-tuple-element.32.own_ref), channel_id=1, source_target_pairs={{0,1},{1,0},{2,3},{3,2},{4,5},{5,4},{6,7},{7,6},{8,9},{9,8},{10,11... | collective-permute-start | bytes 798728 | tf_op jit(solution)/shard_map/ppermute | solution.py:389
  16.7 1.2 %collective-permute-start.3 = (s32[8,128]{1,0:T(8,128)S(1)}, s32[8,128]{1,0:T(8,128)S(1)}, u32[]{:S(2)}, u32[]{:S(2)}) collective-permute-start(s32[8,128]{1,0:T(8,128)S(1)} %get-tuple-element.33.own_ref), channel_id=1, source_target_pairs={{0,2},{2,0},{1,3},{3,1},{4,6},{6,4},{5,7},{7,5},{8,10},{10,8},{9,1... | collective-permute-start | bytes 12296 | tf_op jit(solution)/shard_map/ppermute | solution.py:376
  17.8 4.6 %collective-permute-start.6 = (s32[8,128]{1,0:T(8,128)S(1)}, s32[8,128]{1,0:T(8,128)S(1)}, u32[]{:S(2)}, u32[]{:S(2)}) collective-permute-start(s32[8,128]{1,0:T(8,128)S(1)} %join_keys.1.keys_ref.keys0_ref), channel_id=1, source_target_pairs={{0,24},{8,0},{16,8},{24,16},{1,25},{9,1},{17,9},{25,17},{2,26},{10... | collective-permute-start | bytes 12296 | tf_op jit(solution)/shard_map/ppermute | solution.py:387
  20.9 5.1 %collective-permute-start.5 = (s32[8,128]{1,0:T(8,128)S(1)}, s32[8,128]{1,0:T(8,128)S(1)}, u32[]{:S(2)}, u32[]{:S(2)}) collective-permute-start(s32[8,128]{1,0:T(8,128)S(1)} %join_keys.1.keys_ref.keys0_ref), channel_id=1, source_target_pairs={{0,16},{8,24},{16,0},{24,8},{1,17},{9,25},{17,1},{25,9},{2,18},{10... | collective-permute-start | bytes 12296 | tf_op jit(solution)/shard_map/ppermute | solution.py:387
  21.5 4.8 %collective-permute-start.4 = (s32[8,128]{1,0:T(8,128)S(1)}, s32[8,128]{1,0:T(8,128)S(1)}, u32[]{:S(2)}, u32[]{:S(2)}) collective-permute-start(s32[8,128]{1,0:T(8,128)S(1)} %join_keys.1.keys_ref.keys0_ref), channel_id=1, source_target_pairs={{0,8},{8,16},{16,24},{24,0},{1,9},{9,17},{17,25},{25,1},{2,10},{10... | collective-permute-start | bytes 12296 | tf_op jit(solution)/shard_map/ppermute | solution.py:387
  30.4 9.8 %copy-start.2 = (bf16[16,136,128]{2,1,0:T(8,128)(2,1)}, bf16[16,136,128]{2,1,0:T(8,128)(2,1)S(1)}, u32[]{:S(2)}) copy-start(bf16[16,136,128]{2,1,0:T(8,128)(2,1)S(1)} %all-to-all-done.1.ring_ref) | copy-start | bytes 1671172
  32.4 13.5 %all-to-all-start.2 = ((bf16[8,264,128]{2,1,0:T(8,128)(2,1)}), bf16[8,264,128]{2,1,0:T(8,128)(2,1)S(1)}, u32[]{:S(2)}, u32[]{:S(2)}) async-start(bf16[8,264,128]{2,1,0:T(8,128)(2,1)} %select.1), calls=%async_computation.2 | async-start | bytes 1081344 | tf_op jit(solution)/shard_map/all_to_all | solution.py:406
  38.6 1.5 %collective-permute-start = (bf16[1040,128]{1,0:T(8,128)(2,1)S(1)}, bf16[1040,128]{1,0:T(8,128)(2,1)S(1)}, u32[]{:S(2)}, u32[]{:S(2)}) collective-permute-start(bf16[1040,128]{1,0:T(8,128)(2,1)S(1)} %get-tuple-element.32.own_ref), channel_id=1, source_target_pairs={{0,2},{2,0},{1,3},{3,1},{4,6},{6,4},{5,7},{7,5},{8,10},{10,8},{9,1... | collective-permute-start | bytes 798728 | tf_op jit(solution)/shard_map/ppermute | solution.py:388
  38.6 1.9 %collective-permute-start.2 = (bf16[1040,128]{1,0:T(8,128)(2,1)S(1)}, bf16[1040,128]{1,0:T(8,128)(2,1)S(1)}, u32[]{:S(2)}, u32[]{:S(2)}) collective-permute-start(bf16[1040,128]{1,0:T(8,128)(2,1)S(1)} %collective-permute-done.1.lay_ref), channel_id=1, source_target_pairs={{0,2},{2,0},{1,3},{3,1},{4,6},{6,4},{5,7},{7,5},{8,10},{10,8},{9,1... | collective-permute-start | bytes 798728 | tf_op jit(solution)/shard_map/ppermute | solution.py:408
